TPU v7x, 128 devices: a whole 4x4x4 slice. The times are simulated.
128 devices in a mesh: expert: 32 (over x, y, z_lo), tensor: 4 (over z_hi, core).
Axes of the slice: x: 4, y: 4, z: 4 (z_hi: 2, z_lo: 2; z = z_hi * 2 + z_lo), core: 2. Of those that a mesh axis runs over, the one named last changes fastest.
Arguments:
- tokens: bfloat16 [4096, 2560], P('expert', 'tensor'), may hold values from -6 to 6
- slot: int32 [4096, 1], P('expert'), may hold values from 0 to 63; in each aligned block of 128 rows (0 to 127, 128 to 255, ...) at most 4 rows name the same one
- mask: int32 [4096], P('expert'), may hold values 0 or 1
- hot_group: int32 [1], replicated, may hold values from 0 to 31
- router_weight: bfloat16 [2560, 32], replicated, may hold values from -0.125 to 0.125
- exp_gate: bfloat16 [32, 2560, 4096], P('expert', None, 'tensor'), may hold values from -0.125 to 0.125
- exp_up: bfloat16 [32, 2560, 4096], P('expert', None, 'tensor'), may hold values from -0.125 to 0.125
- exp_down: bfloat16 [32, 4096, 2560], P('expert', 'tensor'), may hold values from -0.09375 to 0.09375
- sh_gate: bfloat16 [2560, 4096], P('expert', 'tensor'), may hold values from -0.125 to 0.125
- sh_up: bfloat16 [2560, 4096], P('expert', 'tensor'), may hold values from -0.125 to 0.125
- sh_down: bfloat16 [4096, 2560], P('tensor', 'expert'), may hold values from -0.09375 to 0.09375
Outputs:
- mixed: bfloat16 [4096, 2560], P('expert', 'tensor')
Inputs may be any that keep to these rules, and one draw needn't show every extreme that they name: Slot 2 g is the home slot of expert g, slot 2 g + 1 the spare slot of group g. Among the 128 tokens of one group no slot is named by more than 4 tokens, a bound that some block reaches.
All inputs are finite; a program needn't handle non-finite values. No bound on the sum of `mask` on one device may be relied on, other than what follows from the above.
Results may differ from a plain program's by a relative error of at most 0.0052.
Values may be sent and summed in bfloat16 or wider, within the bound.
A program may use at most 192 MiB of HBM per device.

v0:
```python
import jax
import jax.numpy as jnp
from jax import lax
from jax.sharding import PartitionSpec as P


def side_by_side(arrays, axis, dim, along):
    ends, at = ([], 0)
    for a in arrays[:-1]:
        at += a.shape[along]
        ends.append(at)
    both = jnp.concatenate(arrays, axis=along)
    return tuple(jnp.split(lax.all_gather(both, axis, axis=dim, tiled=True), ends, axis=along))


def from_root(block, axis, source):
    block = jnp.where(lax.axis_index(axis) == source, block, jnp.zeros_like(block))
    return lax.psum(block, axis)


def cut_along(array, dim, length):
    before, after = (array.shape[:dim], array.shape[dim + 1 :])
    return jnp.moveaxis(array.reshape(*before, length, -1, *after), dim, 0)


def sent_and_summed(array, axis, dim):
    tiles = cut_along(array, dim, lax.axis_size(axis))
    arrived = lax.all_to_all(tiles, axis, split_axis=0, concat_axis=0, tiled=True)
    return arrived.sum(axis=0)


def expert_ffn(batch_rows, w_gate, w_up, w_down):
    gated = jnp.dot(batch_rows, w_gate, preferred_element_type=jnp.float32)
    upward = jnp.dot(batch_rows, w_up, preferred_element_type=jnp.float32)
    hidden = (jax.nn.silu(gated) * upward).astype(jnp.bfloat16)
    return jnp.dot(hidden, w_down, preferred_element_type=jnp.float32)


def local(
    tokens,
    slot,
    mask,
    hot_group,
    router_weight,
    exp_gate,
    exp_up,
    exp_down,
    sh_gate,
    sh_up,
    sh_down,
):
    n_groups = lax.axis_size("expert")
    whole = lax.all_gather(tokens, "tensor", axis=1, tiled=True)
    tok_count = whole.shape[0]
    width = whole.shape[1]
    capacity = tok_count // n_groups
    slot_count = 2 * n_groups
    slot_ids = slot[:, 0]
    hot_index = hot_group[0]
    expert_id = jnp.where(slot_ids % 2 == 0, slot_ids // 2, hot_index)
    logits = jnp.dot(whole, router_weight, preferred_element_type=jnp.float32)
    chosen = expert_id[:, None] == lax.broadcasted_iota(jnp.int32, (1, router_weight.shape[1]), 1)
    weighting = jax.nn.sigmoid(jnp.sum(jnp.where(chosen, logits, 0.0), axis=1))
    pieces = side_by_side((sh_gate, sh_up), "expert", 0, 1)
    shared_gate = jnp.dot(whole, pieces[0], preferred_element_type=jnp.float32)
    shared_up = jnp.dot(whole, pieces[1], preferred_element_type=jnp.float32)
    sh_hidden = (jax.nn.silu(shared_gate) * shared_up).astype(jnp.bfloat16)
    shared_terms = jnp.dot(
        sh_hidden,
        lax.all_gather(sh_down, "expert", axis=1, tiled=True),
        preferred_element_type=jnp.float32,
    )
    shared = lax.psum_scatter(shared_terms, "tensor", scatter_dimension=1, tiled=True)
    slot_hits = (slot_ids[:, None] == lax.broadcasted_iota(jnp.int32, (1, slot_count), 1)).astype(
        jnp.int32
    )
    position = jnp.sum((jnp.cumsum(slot_hits, axis=0) - 1) * slot_hits, axis=1)
    target = slot_ids * capacity + position
    placing = (
        lax.broadcasted_iota(jnp.int32, (slot_count * capacity, 1), 0) == target[None, :]
    ).astype(jnp.bfloat16)
    outgoing = jnp.dot(placing, tokens, preferred_element_type=jnp.float32).astype(jnp.bfloat16)
    quarter = lax.all_to_all(outgoing, "expert", split_axis=0, concat_axis=0, tiled=True)
    arrived = lax.all_gather(quarter, "tensor", axis=1, tiled=True)
    replica = (
        from_root(exp_gate[0], "expert", hot_index),
        from_root(exp_up[0], "expert", hot_index),
        from_root(exp_down[0], "expert", hot_index),
    )
    grouped = arrived.reshape(n_groups, 2, capacity, width)
    home_rows = grouped[:, 0].reshape(n_groups * capacity, width)
    spare_rows = grouped[:, 1].reshape(n_groups * capacity, width)
    home_part = expert_ffn(home_rows, exp_gate[0], exp_up[0], exp_down[0])
    spare_part = expert_ffn(spare_rows, replica[0], replica[1], replica[2])
    partials = jnp.stack(
        [
            home_part.reshape(n_groups, capacity, width),
            spare_part.reshape(n_groups, capacity, width),
        ],
        axis=1,
    )
    partials = partials.reshape(slot_count * capacity, width)
    summed = sent_and_summed(partials, "tensor", 1).astype(jnp.bfloat16)
    returned = lax.all_to_all(summed, "expert", split_axis=0, concat_axis=0, tiled=True)
    routed = lax.dot_general(
        placing, returned, (((0,), (0,)), ((), ())), preferred_element_type=jnp.float32
    )
    keep_rows = mask.astype(jnp.float32)
    mixed = keep_rows[:, None] * (shared + weighting[:, None] * routed)
    return mixed.astype(jnp.bfloat16)


def solution(mesh):
    in_specs = (
        P("expert", "tensor"),
        P("expert", None),
        P("expert"),
        P(),
        P(),
        P("expert", None, "tensor"),
        P("expert", None, "tensor"),
        P("expert", "tensor", None),
        P("expert", "tensor"),
        P("expert", "tensor"),
        P("tensor", "expert"),
    )
    out_specs = P("expert", "tensor")
    return jax.shard_map(local, mesh=mesh, in_specs=in_specs, out_specs=out_specs, check_vma=False)
```

profile of v0, /device:TPU:1, one launch (start us, length us, event | category | flops | bytes accessed | tf_op | source)
XLA Modules:
  0.0 1153.8 jit_solution(9534835826573688970)
XLA Ops:
  7.4 0.8 fusion.57
  8.3 0.8 select_reduce_fusion
  9.8 1.9 fusion.33
  11.7 9.2 all-to-all-start
  21.6 7.7 all-to-all-done
  29.3 0.8 copy-done.3
  30.2 5.1 bitcast_select_fusion
  35.3 8.8 bitcast_select_fusion.1
  44.2 0.8 copy-done.5
  45.1 0.8 pad_maximum_fusion.1
  46.0 0.7 all-gather.6.cloned.1.call-update
  46.7 19.5 %all_gather.13 = bf16[128,2560]{1,0:T(8,128)(2,1)} all-gather(bf16[128,640]{1,0:T(8,128)(2,1)S(1)} %copy-done.4), channel_id=1, replica_groups=mesh['expert'=32,'tensor'=4] {'tensor'}, dimensions={1}, use_global_device_ids=true | all-gather | bytes 819200 | tf_op jit(solution)/shard_map/all_gather | solution.py:53
  66.2 2.8 reshape.30
  69.8 4.6 fusion.8
  74.4 4.6 fusion.25
  79.3 3.4 fusion.10
  82.7 962.7 %all-reduce.3.cloned.1.call-done = (bf16[1024,2560]{1,0:T(8,128)(2,1)}, bf16[2560,1024]{1,0:T(8,128)(2,1)}, bf16[2560,1024]{1,0:T(8,128)(2,1)}) async-done(((bf16[1024,2560]{1,0:T(8,128)(2,1)}, bf16[2560,1024]{1,0:T(8,128)(2,1)}, bf16[2560,1024]{1,0:T(8,128)(2,1)}), (bf16[1024,2560]{1,0:T(8,128)(2,1)}, bf16[2560,1024]{1,0:T(8,128)(2,1)}, bf16[2560,1024]{1,0:T(8,128)(2,1)})) %all-reduce.3.cloned.1.call-update) | async-done | bytes 15728656 | tf_op jit(solution)/shard_map/psum | solution.py:18
  1045.4 5.4 fusion.62
  1050.8 7.7 fusion.40
  1058.6 1.4 stack_reshape.4
  1060.0 1.8 copy.35
  1061.9 5.3 fusion.13
  1067.1 10.9 fusion.38
  1078.3 1.7 copy.36
  1080.0 2.6 reshape_reshape.3
  1082.6 3.5 copy.37
  1086.1 6.0 all-to-all-start.1
  1092.1 38.9 %all-to-all-done.1 = f32[4,256,640]{2,1,0:T(8,128)S(1)} async-done(((f32[4,256,640]{2,1,0:T(8,128)}), f32[4,256,640]{2,1,0:T(8,128)S(1)}, u32[]{:S(2)}, u32[]{:S(2)}) %all-to-all-start.1) | async-done | bytes 2621472 | tf_op jit(solution)/shard_map/all_to_all | solution.py:28
  1131.0 0.9 reduce_sum.29
  1131.9 4.5 all-to-all-start.2
  1136.7 8.0 all-to-all-done.2
  1144.8 1.9 fusion.35
  (41 shorter events, 2.8 us)
Async XLA Ops:
  7.4 1129.0 %copy-start = (bf16[2560,32]{0,1:T(8,128)(2,1)S(1)}, bf16[2560,32]{0,1:T(8,128)(2,1)}, u32[]{:S(2)}) copy-start(bf16[2560,32]{0,1:T(8,128)(2,1)} %param.15) | copy-start | bytes 491524
  11.7 17.6 %all-to-all-start = ((bf16[32,8,640]{2,1,0:T(8,128)(2,1)}), bf16[32,8,640]{2,1,0:T(8,128)(2,1)S(1)}, u32[]{:S(2)}, u32[]{:S(2)}) async-start(bf16[32,8,640]{2,1,0:T(8,128)(2,1)} %fusion.33), calls=%async_computation.1 | async-start | bytes 655360 | tf_op jit(solution)/shard_map/all_to_all | solution.py:83
  20.9 45.3 %all-gather.8.cloned.1.call-start = ((), (), s32[]{:S(2)}) async-start(), calls=%async_computation.7 | async-start | bytes 1638400 | tf_op jit(solution)/shard_map/all_gather | solution.py:84
  29.3 0.8 copy-start.3
  30.1 1015.3 %all-reduce.3.cloned.1.call-start = ((), (), s32[]{:S(2)}) async-start(), calls=%async_computation.8 | async-start | bytes 31457280 | tf_op jit(solution)/shard_map/psum | solution.py:18
  44.1 0.9 copy-start.5
  44.1 1.0 copy-start.6
  44.1 2.6 copy-start.4
  44.2 1017.7 %all-gather.4.cloned.1.call-start = ((), (), s32[]{:S(2)}) async-start(), calls=%async_computation.4 | async-start | bytes 10813440 | tf_op jit(solution)/shard_map/all_gather | solution.py:13
  45.9 1021.2 %all-gather.6.cloned.1.call-start = ((), (), s32[]{:S(2)}) async-start(), calls=%async_computation.5 | async-start | bytes 5406720 | tf_op jit(solution)/shard_map/all_gather | solution.py:70
  46.7 1098.1 %reduce-scatter.2.cloned.1.call-start = ((), (), s32[]{:S(2)}) async-start(), calls=%async_computation.6 | async-start | bytes 1638400 | tf_op jit(solution)/shard_map/reduce_scatter | solution.py:73
  1060.0 7.1 copy-start.1
  1082.6 9.4 copy-start.8
  1082.6 9.4 copy-start.7
  1086.1 50.3 %copy-start.2 = (bf16[128,2560]{1,0:T(8,128)(2,1)S(1)}, bf16[128,2560]{1,0:T(8,128)(2,1)}, u32[]{:S(2)}) copy-start(bf16[128,2560]{1,0:T(8,128)(2,1)} %all_gather.13) | copy-start | bytes 1966084
  1086.1 44.9 %all-to-all-start.1 = ((f32[4,256,640]{2,1,0:T(8,128)}), f32[4,256,640]{2,1,0:T(8,128)S(1)}, u32[]{:S(2)}, u32[]{:S(2)}) async-start(f32[4,256,640]{2,1,0:T(8,128)} %copy.37), calls=%async_computation.2 | async-start | bytes 5242880 | tf_op jit(solution)/shard_map/all_to_all | solution.py:28
  1131.9 12.9 %all-to-all-start.2 = ((bf16[32,8,640]{2,1,0:T(8,128)(2,1)}), bf16[32,8,640]{2,1,0:T(8,128)(2,1)S(1)}, u32[]{:S(2)}, u32[]{:S(2)}) async-start(bf16[32,8,640]{2,1,0:T(8,128)(2,1)} %bitcast.62), calls=%async_computation.3 | async-start | bytes 655360 | tf_op jit(solution)/shard_map/all_to_all | solution.py:104
Sparse Core Ops, SparseCore 0:
  30.3 22.9 all-gather.7
  54.9 517.1 all-gather.3
  573.8 422.2 all-gather.5
  1078.2 40.1 reduce-scatter.1
Sparse Core Ops, SparseCore 1:
  44.2 1001.1 all-reduce.2
where the time goes:
time: 1160 us; the launch traced here: 1150 us
  waiting for transfers between devices  1020 us (88%)
  matrix products  46.1 us (4%)
  starting transfers between devices  19.8 us (2%)
  blocking collectives  19.5 us (2%)
  other arithmetic  18.3 us (2%)
  local copies, waits for them, and re-layouts  16.5 us (1%)
  between operations  15.4 us (1%)
    psum x1, waiting for transfers between devices, from_root(): return lax.psum(block, axis)  963 us
    all_to_all x1, waiting for transfers between devices, sent_and_summed(): lax.all_to_all(tiles, axis, split_axis=0, concat_axis=0, tiled=True)  38.9 us
  transfers between devices with their start and end apart: 8, of which 4 were waited for; matrix products, arithmetic and copies ran while one was open for 5% of the time, Pallas kernels for 0%

commit v1 on v0

v1 whole, which is shorter than its diff:
```python
import functools

import jax
import jax.numpy as jnp
from jax import lax
from jax.experimental import pallas as pl
from jax.experimental.pallas import tpu as pltpu
from jax.sharding import PartitionSpec as P

MESH = pl.DeviceIdType.MESH
NX, NY, NZ, NT, CAP = 4, 4, 2, 4, 4


def coords():
    e = lax.axis_index("expert")
    return lax.div(e, NY * NZ), lax.rem(lax.div(e, NZ), NY), lax.rem(e, NZ)


def group_of(x, y, z):
    return (x * NY + y) * NZ + z


def turn(i, n=4):
    return lax.rem(i + 2 * n, n)


class Copies:
    def __init__(self, send, recv, local):
        self.send, self.recv, self.local = send, recv, local
        self.sent, self.kept = 0, 0
        self.started = []

    def remote(self, src, dst, device):
        c = pltpu.make_async_remote_copy(
            src_ref=src,
            dst_ref=dst,
            send_sem=self.send.at[self.sent],
            recv_sem=self.recv.at[self.sent],
            device_id=device,
            device_id_type=MESH,
        )
        self.sent += 1
        c.start()
        self.started.append(c)
        return c

    def here(self, src, dst):
        c = pltpu.make_async_copy(src, dst, self.local.at[self.kept])
        self.kept += 1
        c.start()
        return c


def entry_barrier(devices):
    barrier = pltpu.get_barrier_semaphore()
    for d in devices:
        pl.semaphore_signal(barrier, inc=1, device_id=d, device_id_type=MESH)
    pl.semaphore_wait(barrier, len(devices))


def choose(flag, rows, step, mine, into):
    def body(i, carry):
        at = pl.ds(pl.multiple_of(i * step, step), step)
        into[at] = jnp.where(flag == 1, mine(at), into[at])
        return carry

    lax.fori_loop(0, rows // step, body, 0)


def spread_kernel(
    flags, gate, up, down, sh_own, tok,
    hg, hu, hd, sh, tk,
    own_g, own_u, own_d, xg, xu, yg, yu, yd, xd, zg, zu, zd,
    send, recv, local,
):
    x, y, z = coords()
    t = lax.axis_index("tensor")
    cp = Copies(send, recv, local)
    rows, cols = xg.shape[2], xg.shape[3]
    quarter = tok.shape[1]

    def at(dx=0, dy=0, dz=0):
        return {"expert": group_of(turn(x + dx), turn(y + dy), turn(z + dz, 2)), "tensor": t}

    def peer(dt):
        return {"expert": group_of(x, y, z), "tensor": turn(t + dt)}

    entry_barrier(
        [at(1), at(-1), at(2), at(0, 1), at(0, -1), at(0, 0, 1), peer(1), peer(2), peer(3)]
    )
    fx, fy, fz = flags[0], flags[1], flags[2]

    streams = ((gate, own_g, xg, yg, zg, hg, 1), (up, own_u, xu, yu, zu, hu, -1))

    def block(sign, j):
        return turn(y - sign * (1 + j))

    def piece(ref, sign, j, xp):
        return ref.at[
            pl.ds(pl.multiple_of(block(sign, j) * rows, rows), rows),
            pl.ds(pl.multiple_of(xp * cols, cols), cols),
        ]

    x_copy = {}

    def x_first(j):
        for s, (w, _, xb, _, _, _, sign) in enumerate(streams):
            x_copy[s, j, 0] = cp.remote(piece(w, sign, j, turn(x - sign)), xb.at[j, 0], at(sign))

    own_copy = {}

    def own_load(j):
        for s, (w, own, _, _, _, _, sign) in enumerate(streams):
            src = w.at[pl.ds(pl.multiple_of(block(sign, j) * rows, rows), rows), :]
            own_copy[s, j] = cp.here(src, own.at[j])

    def x_step(j, step):
        for s, (_, own, xb, _, _, _, sign) in enumerate(streams):
            x_copy[s, j, step].wait_recv()
            if step == 0:
                own_copy[s, j].wait()
            xp = turn(x - sign * (2 + step))
            lanes = pl.ds(pl.multiple_of(xp * cols, cols), cols)
            choose(fx, rows, rows // 4, lambda r, own=own, lanes=lanes: own[j, r, lanes], xb.at[j, step])
            if step < 2:
                x_copy[s, j, step + 1] = cp.remote(xb.at[j, step], xb.at[j, step + 1], at(sign))

    y_copy = {}

    def y_step(j):
        for s, (_, _, xb, yb, _, _, sign) in enumerate(streams):
            if j == 0:
                y_copy[s, 0] = cp.remote(xb.at[0, 2], yb.at[0], at(0, sign))
                continue
            y_copy[s, j - 1].wait_recv()
            choose(fy, rows, rows // 4, lambda r, xb=xb: xb[j, 2, r], yb.at[j - 1])
            if j < 3:
                y_copy[s, j] = cp.remote(yb.at[j - 1], yb.at[j], at(0, sign))

    d_copy = {}

    def d_first():
        for r, sign in ((0, 1), (1, -1)):
            d_copy[r, 0] = cp.remote(down.at[:, turn(y - sign), r], yd.at[r, 0], at(0, sign))

    def d_step(step):
        for r, sign in ((0, 1), (1, -1)):
            d_copy[r, step].wait_recv()
            yp = turn(y - sign * (2 + step))
            choose(fy, NX, 1, lambda i, yp=yp, r=r: own_d[i, yp, r], yd.at[r, step])
            if step < 2:
                d_copy[r, step + 1] = cp.remote(yd.at[r, step], yd.at[r, step + 1], at(0, sign))

    dx_copy = {}

    def dx_step(step):
        for r, sign in ((0, 1), (1, -1)):
            if step == 0:
                dx_copy[r, 0] = cp.remote(yd.at[r, 2, turn(x - sign)], xd.at[r, 0], at(sign))
                continue
            dx_copy[r, step - 1].wait_recv()
            xp = turn(x - sign * (1 + step))
            n = xd.shape[2]
            choose(fx, n, 16, lambda i, xp=xp, r=r: yd[r, 2, xp, i], xd.at[r, step - 1])
            if step < 3:
                dx_copy[r, step] = cp.remote(xd.at[r, step - 1], xd.at[r, step], at(sign))

    x_first(0)
    d_first()
    own_load(0)
    own_d_copy = cp.here(down, own_d)
    k = sh_own.shape[1]

    def sh_piece(xp):
        return sh_own.at[:, :, pl.ds(pl.multiple_of(xp * cols, cols), cols)]

    s_x = [
        cp.remote(sh_piece(turn(x + d)), sh.at[:, x, y, z], at(d)) for d in (1, -1, 2)
    ]
    s_own = cp.here(sh_piece(x), sh.at[:, x, y, z])
    mine = pl.ds(pl.multiple_of(t * quarter, quarter), quarter)
    t_x = [cp.remote(tok, tk.at[x, :, mine], at(d)) for d in (1, -1, 2)]
    t_own = cp.here(tok, tk.at[x, :, mine])
    x_first(1)
    own_load(1)
    own_load(2)
    own_load(3)

    x_step(0, 0)
    for c in t_x:
        c.wait_recv()
    t_own.wait()
    t_t = [cp.remote(tk.at[:, :, mine], tk.at[:, :, mine], peer(d)) for d in (1, 2, 3)]
    for c in s_x:
        c.wait_recv()
    s_own.wait()
    s_y = [cp.remote(sh.at[:, :, y, z], sh.at[:, :, y, z], at(0, d)) for d in (1, -1)]
    s_z = [cp.remote(sh.at[:, :, y, z], sh.at[:, :, y, z], at(0, 0, 1))]
    x_step(1, 0)
    own_d_copy.wait()
    d_step(0)
    x_step(0, 1)
    x_step(1, 1)
    x_first(2)
    x_first(3)
    for c in s_y:
        c.wait_recv()
    lo, hi = turn(y - 1), turn(y + 1)
    s_y2 = [
        cp.remote(sh.at[:, 0:2, lo, z], sh.at[:, 0:2, lo, z], at(0, 1)),
        cp.remote(sh.at[:, 2:4, hi, z], sh.at[:, 2:4, hi, z], at(0, -1)),
    ]
    s_z += [cp.remote(sh.at[:, :, v, z], sh.at[:, :, v, z], at(0, 0, 1)) for v in (lo, hi)]
    d_step(1)
    x_step(0, 2)
    y_step(0)
    x_step(1, 2)
    y_step(1)
    d_step(2)
    dx_step(0)
    for c in s_y2:
        c.wait_recv()
    far = turn(y + 2)
    s_z.append(cp.remote(sh.at[:, :, far, z], sh.at[:, :, far, z], at(0, 0, 1)))
    x_step(2, 0)
    dx_step(1)
    x_step(3, 0)
    dx_step(2)
    x_step(2, 1)
    dx_step(3)
    d_z = [cp.remote(xd.at[r, 2], zd.at[r], at(0, 0, 1)) for r in (0, 1)]
    x_step(3, 1)
    d_y, d_own = [], []
    for r in (0, 1):
        d_z[r].wait_recv()
        choose(fz, zd.shape[1], 16, lambda i, r=r: xd[r, 2, i], zd.at[r])
        d_own.append(cp.here(zd.at[r], hd.at[y, r]))
        d_y.append([cp.remote(zd.at[r], hd.at[y, r], at(0, d)) for d in (1, -1)])
    x_step(2, 2)
    y_step(2)
    d_y[0][0].wait_recv()
    d_y[1][1].wait_recv()
    d_y2 = [
        cp.remote(hd.at[lo, 0], hd.at[lo, 0], at(0, 1)),
        cp.remote(hd.at[hi, 1], hd.at[hi, 1], at(0, -1)),
    ]
    x_step(3, 2)
    y_step(3)
    z_copy = [cp.remote(st[3].at[2], st[4], at(0, 0, 1)) for st in streams]
    a_own, a_y = [], []

    def rows_of(ref, v):
        return ref.at[pl.ds(pl.multiple_of(v * rows, rows), rows)]

    for s, (_, _, _, yb, zb, h, sign) in enumerate(streams):
        z_copy[s].wait_recv()
        choose(fz, rows, rows // 4, lambda r, yb=yb: yb[2, r], zb)
        a_own.append(cp.here(zb, rows_of(h, y)))
        a_y.append([cp.remote(zb, rows_of(h, y), at(0, d)) for d in (sign, -sign)])
    a_y2 = []
    for s, st in enumerate(streams):
        h, sign = st[5], st[6]
        a_y[s][0].wait_recv()
        v = turn(y - sign)
        a_y2.append(cp.remote(rows_of(h, v), rows_of(h, v), at(0, sign)))
    for c in t_t + s_z + d_y2:
        c.wait_recv()
    d_y[0][1].wait_recv()
    d_y[1][0].wait_recv()
    for s in (0, 1):
        a_y[s][1].wait_recv()
        a_y2[s].wait_recv()
    for c in d_own + a_own:
        c.wait()
    for c in cp.started:
        c.wait_send()


def spread(flags, gate, up, down, sh_own, tok):
    d, h = gate.shape
    rows, cols = d // NY, h // NX
    part = cols // (2 * NY)
    down = down.reshape(NX, NY, 2, part, d)
    bf = jnp.bfloat16
    any_spec = pl.BlockSpec(memory_space=pl.ANY)
    return pl.pallas_call(
        spread_kernel,
        out_shape=[
            jax.ShapeDtypeStruct((d, cols), bf),
            jax.ShapeDtypeStruct((d, cols), bf),
            jax.ShapeDtypeStruct((NY, 2, part, d), bf),
            jax.ShapeDtypeStruct((3, NX, NY, NZ, sh_own.shape[1], cols), bf),
            jax.ShapeDtypeStruct((NX, tok.shape[0], NT * tok.shape[1]), bf),
        ],
        in_specs=[pl.BlockSpec(memory_space=pltpu.SMEM)] + [any_spec] * 5,
        out_specs=[any_spec] * 5,
        scratch_shapes=[
            pltpu.VMEM((NY, rows, h), bf),
            pltpu.VMEM((NY, rows, h), bf),
            pltpu.VMEM((NX, NY, 2, part, d), bf),
            pltpu.VMEM((NY, 3, rows, cols), bf),
            pltpu.VMEM((NY, 3, rows, cols), bf),
            pltpu.VMEM((3, rows, cols), bf),
            pltpu.VMEM((3, rows, cols), bf),
            pltpu.VMEM((2, 3, NX, part, d), bf),
            pltpu.VMEM((2, 3, part, d), bf),
            pltpu.VMEM((rows, cols), bf),
            pltpu.VMEM((rows, cols), bf),
            pltpu.VMEM((2, part, d), bf),
            pltpu.SemaphoreType.DMA((80,)),
            pltpu.SemaphoreType.DMA((80,)),
            pltpu.SemaphoreType.DMA((20,)),
        ],
        compiler_params=pltpu.CompilerParams(
            collective_id=0, has_side_effects=True, vmem_limit_bytes=44 * 2**20
        ),
    )(flags, gate, up, down, sh_own, tok)


def sum_kernel(part, out, kept, from_core, mid, from_x, half, from_z, send, recv, local):
    x, y, z = coords()
    t = lax.axis_index("tensor")
    core, z_hi = lax.rem(t, 2), lax.div(t, 2)
    g = group_of(x, y, z)
    cp = Copies(send, recv, local)
    n, width = from_x.shape[1], from_x.shape[2]
    quarter = width // 2
    other = {"expert": g, "tensor": z_hi * 2 + (1 - core)}
    across = {"expert": g, "tensor": (1 - z_hi) * 2 + core}

    def at(dx):
        return {"expert": group_of(turn(x + dx), y, z), "tensor": t}

    entry_barrier([other, across, at(1), at(-1), at(2)])
    order = (2, 1, 3, 0)
    c_copy, k_copy = [], []
    for d in order:
        xp = turn(x + d)
        c_copy.append(
            cp.remote(part.at[xp, 1 - core], from_core.at[d], other)
        )
        k_copy.append(cp.here(part.at[xp, core], kept.at[d]))
    x_copy = []
    for i, d in enumerate(order):
        c_copy[i].wait_recv()
        k_copy[i].wait()

        def body(r, carry, d=d):
            a = pl.ds(pl.multiple_of(r * 32, 32), 32)
            mid[d, a] = (
                kept[d, a].astype(jnp.float32) + from_core[d, a].astype(jnp.float32)
            ).astype(mid.dtype)
            return carry

        lax.fori_loop(0, n // 32, body, 0)
        if d:
            x_copy.append(cp.remote(mid.at[d], from_x.at[(d - 1)], at(d)))
    for c in x_copy:
        c.wait_recv()
    away = pl.ds(pl.multiple_of((1 - z_hi) * quarter, quarter), quarter)
    own = pl.ds(pl.multiple_of(z_hi * quarter, quarter), quarter)

    def total(a, lanes):
        v = kept[0, a, lanes].astype(jnp.float32) + from_core[0, a, lanes].astype(jnp.float32)
        for i in range(3):
            v += from_x[i, a, lanes].astype(jnp.float32)
        return v

    def body2(r, carry):
        a = pl.ds(pl.multiple_of(r * 32, 32), 32)
        half[a] = total(a, away).astype(half.dtype)
        return carry

    lax.fori_loop(0, n // 32, body2, 0)
    z_copy = cp.remote(half, from_z, across)
    z_copy.wait_recv()

    def body3(r, carry):
        a = pl.ds(pl.multiple_of(r * 32, 32), 32)
        out[a] = total(a, own) + from_z[a].astype(jnp.float32)
        return carry

    lax.fori_loop(0, n // 32, body3, 0)
    for c in cp.started:
        c.wait_send()


def summed(part):
    _, _, n, width = part.shape
    bf = jnp.bfloat16
    return pl.pallas_call(
        sum_kernel,
        out_shape=jax.ShapeDtypeStruct((n, width // 2), jnp.float32),
        in_specs=[pl.BlockSpec(memory_space=pl.ANY)],
        out_specs=pl.BlockSpec(memory_space=pltpu.VMEM),
        scratch_shapes=[
            pltpu.VMEM((NX, n, width), bf),
            pltpu.VMEM((NX, n, width), bf),
            pltpu.VMEM((NX, n, width), bf),
            pltpu.VMEM((3, n, width), bf),
            pltpu.VMEM((n, width // 2), bf),
            pltpu.VMEM((n, width // 2), bf),
            pltpu.SemaphoreType.DMA((10,)),
            pltpu.SemaphoreType.DMA((10,)),
            pltpu.SemaphoreType.DMA((5,)),
        ],
        compiler_params=pltpu.CompilerParams(
            collective_id=1, has_side_effects=True, vmem_limit_bytes=24 * 2**20
        ),
    )(part)


def dot(a, b):
    return jnp.dot(a, b, preferred_element_type=jnp.float32)


def hidden_units(rows, w_gate, w_up):
    return jax.nn.silu(dot(rows, w_gate)) * dot(rows, w_up)


def local(
    tokens, slot, mask, hot_group, router_weight,
    exp_gate, exp_up, exp_down, sh_gate, sh_up, sh_down,
):
    n_groups = lax.axis_size("expert")
    bf = jnp.bfloat16
    x, y, z = coords()
    hot = hot_group[0]
    hx, hy, hz = hot // (NY * NZ), (hot // NZ) % NY, hot % NZ
    flags = jnp.stack([hx == x, hy == y, hz == z]).astype(jnp.int32)
    quads = [[(a * NY + b) * NZ + c for a in range(NX)] for b in range(NY) for c in range(NZ)]
    n = tokens.shape[0]

    whole = lax.all_gather(tokens, "tensor", axis=1, tiled=True)
    ids = slot[:, 0]
    same = ids[:, None] == ids[None, :]
    earlier = lax.broadcasted_iota(jnp.int32, (n, n), 1) < lax.broadcasted_iota(jnp.int32, (n, n), 0)
    position = jnp.sum((same & earlier).astype(jnp.int32), axis=1)
    target = jnp.where(ids % 2 == 0, (ids // 2) * CAP + position, -1)
    placing = lax.broadcasted_iota(jnp.int32, (n_groups * CAP, 1), 0) == target[None, :]
    outgoing = dot(placing.astype(bf), whole).astype(bf)
    arrived = lax.all_to_all(outgoing, "expert", split_axis=0, concat_axis=0, tiled=True)
    home_hidden = hidden_units(arrived, exp_gate[0], exp_up[0]).astype(bf)
    home_part = dot(home_hidden, exp_down[0]).astype(bf)
    returned = lax.all_to_all(home_part, "expert", split_axis=0, concat_axis=0, tiled=True)

    sh_own = jnp.stack([sh_gate, sh_up, sh_down.T])
    hot_gate, hot_up, hot_down, sh, quad_tokens = spread(
        flags, exp_gate[0], exp_up[0], exp_down[0], sh_own, tokens
    )
    d = hot_gate.shape[0]
    hot_down = hot_down.reshape(-1, d)
    sh = sh.reshape(3, d, -1)
    quad_tokens = quad_tokens.reshape(NX * n, d)
    quad_ids = lax.all_gather(ids, "expert", axis_index_groups=quads).reshape(-1)
    expert_id = jnp.where(quad_ids % 2 == 0, quad_ids // 2, hot)
    logits = dot(quad_tokens, router_weight)
    chosen = expert_id[:, None] == lax.broadcasted_iota(jnp.int32, (1, router_weight.shape[1]), 1)
    weighting = jax.nn.sigmoid(jnp.sum(jnp.where(chosen, logits, 0.0), axis=1))
    spare = jnp.where(quad_ids % 2 == 1, weighting, 0.0)

    sh_hidden = hidden_units(quad_tokens, sh[0], sh[1]).astype(bf)
    hot_hidden = (hidden_units(quad_tokens, hot_gate, hot_up) * spare[:, None]).astype(bf)
    part = lax.dot_general(
        sh_hidden, sh[2], (((1,), (1,)), ((), ())), preferred_element_type=jnp.float32
    ) + dot(hot_hidden, hot_down)
    back = lax.dot_general(
        placing.astype(bf), returned, (((0,), (0,)), ((), ())), preferred_element_type=jnp.float32
    )
    own_weighting = lax.dynamic_slice_in_dim(weighting, x * n, n)
    here = (lax.broadcasted_iota(jnp.int32, (NX, 1, 1), 0) == x).astype(jnp.float32)
    part = part.reshape(NX, n, d) + here * (own_weighting[:, None] * back)[None]
    part = part.astype(bf).reshape(NX, n, 2, 2, d // 4)
    part = part.transpose(0, 3, 1, 2, 4).reshape(NX, 2, n, d // 2)
    mixed = mask.astype(jnp.float32)[:, None] * summed(part)
    return mixed.astype(bf)


def solution(mesh):
    in_specs = (
        P("expert", "tensor"),
        P("expert", None),
        P("expert"),
        P(),
        P(),
        P("expert", None, "tensor"),
        P("expert", None, "tensor"),
        P("expert", "tensor", None),
        P("expert", "tensor"),
        P("expert", "tensor"),
        P("tensor", "expert"),
    )
    out_specs = P("expert", "tensor")
    return jax.shard_map(local, mesh=mesh, in_specs=in_specs, out_specs=out_specs, check_vma=False)
```

time: 1160 us -> 277 us (0.24)
  waiting for transfers between devices: 1020 us -> 0.01 us
  Pallas kernels: 0 us -> 181 us
  matrix products: 46.1 us -> 30.8 us
  between operations: 15.4 us -> 0.9 us
  other arithmetic: 18.3 us -> 5.75 us
    psum x1 -> x0, waiting for transfers between devices: 963 us -> none  [from_root(): return lax.psum(block, axis)]
    pallas_call x0 -> x2, Pallas kernels: none -> 181 us  [the longest x1 147 us: spread(): pl.pallas_call(spread_kernel, out_shape=[jax.ShapeDtypeStruct((d, cols),...]
    all_to_all x2 -> x1, waiting for transfers between devices: 47 us -> 0.01 us  [local(): lax.all_to_all(home_part, 'expert', split_axis=0, concat_axis=0, tiled=True)]
    dot_general x10 -> x9, matrix products: 46.1 us -> 30.8 us  [the longest x7 23.4 us: dot(): return jnp.dot(a, b, preferred_element_type=jnp.float32)]
    select_n x2, other arithmetic: 13.9 us -> 0.69 us  [the longest x1 0.67 us: local(): target = jnp.where(ids % 2 == 0, ids // 2 * CAP + position, -1)]
  transfers between devices with their start and end apart: 8 -> 2, of which waited for: 4 -> 0; matrix products, arithmetic and copies ran while one was open for 5% -> 11% of each run, Pallas kernels for 0% -> 53%
where the time goes in v1:
time: 277 us; the launch traced here: 276 us
  Pallas kernels  181 us (65%)
  matrix products  30.8 us (11%)
  blocking collectives  22.9 us (8%)
  local copies, waits for them, and re-layouts  20.7 us (7%)
  starting transfers between devices  13.8 us (5%)
  other arithmetic  5.75 us (2%)
    pallas_call x1, Pallas kernels, spread(): pl.pallas_call(spread_kernel, out_shape=[jax.ShapeDtypeStruct((d, cols),...  147 us
    pallas_call x1, Pallas kernels, summed(): pl.pallas_call(sum_kernel, out_shape=jax.ShapeDtypeStruct((n, width // 2)...  34.5 us
    dot_general x7, matrix products, dot(): return jnp.dot(a, b, preferred_element_type=jnp.float32)  23.4 us
    all_gather x1, blocking collectives, local(): whole = lax.all_gather(tokens, 'tensor', axis=1, tiled=True)  11.8 us
    all_gather x1, blocking collectives, local(): lax.all_gather(ids, 'expert', axis_index_groups=quads).reshape(-1)  11.1 us
    all_to_all x1, starting transfers between devices, local(): lax.all_to_all(outgoing, 'expert', split_axis=0, concat_axis=0, tiled=True)  7.61 us
    reshape x1, local copies, waits for them, and re-layouts, local(): part = part.reshape(NX, n, d) + here * (own_weighting[:, None] * back)[None]  7.52 us
    dot_general x1, matrix products, local(): lax.dot_general(sh_hidden, sh[2], (((1,), (1,)), ((), ())), preferred_ele...  7.02 us
  transfers between devices with their start and end apart: 2, of which 0 were waited for; matrix products, arithmetic and copies ran while one was open for 11% of the time, Pallas kernels for 53%

profile of v1, /device:TPU:1, one launch (start us, length us, event | category | flops | bytes accessed | tf_op | source)
XLA Modules:
  0.0 276.2 jit_solution(8488385816459102886)
XLA Ops:
  0.0 0.9 convert_reduce_fusion
  1.0 0.7 compare_select_fusion
  1.7 11.8 %all_gather.7 = bf16[128,2560]{1,0:T(8,128)(2,1)S(1)} all-gather(bf16[128,640]{1,0:T(8,128)(2,1)} %tok.1), channel_id=1, replica_groups=mesh['expert'=32,'tensor'=4] {'tensor'}, dimensions={1}, use_global_device_ids=true | all-gather | bytes 819200 | tf_op jit(solution)/shard_map/all_gather | solution.py:434
  13.5 0.3 convolution_convert_fusion
  13.8 1.0 all_to_all.16
  14.8 7.6 %all-to-all-start = ((bf16[32,4,2560]{2,1,0:T(4,128)(2,1)}), bf16[32,4,2560]{2,1,0:T(4,128)(2,1)}, u32[]{:S(2)}, u32[]{:S(2)}) async-start(bf16[32,4,2560]{2,1,0:T(4,128)(2,1)} %all_to_all.16), calls=%async_computation | async-start | bytes 1310720 | tf_op jit(solution)/shard_map/all_to_all | solution.py:442
  23.1 11.1 %all-gather = s32[512,1]{0,1:T(1,128)S(1)} all-gather(s32[128,1]{0,1:T(1,128)S(1)} %copy-done.7), channel_id=2, replica_groups={{0,32,64,96},{4,36,68,100},{8,40,72,104},{12,44,76,108},{16,48,80,112},..., dimensions={0}, use_global_device_ids=true | all-gather | bytes 2560 | tf_op jit(solution)/shard_map/all_gather | solution.py:455
  34.2 0.1 add_convert_fusion.flags
  34.3 0.1 pad_maximum_fusion.sh_own
  34.4 146.8 %shard_map.109 = (bf16[2560,256]{1,0:T(8,128)(2,1)S(1)}, bf16[2560,256]{1,0:T(8,128)(2,1)S(1)}, bf16[4,2,32,2560]{3,2,1,0:T(8,128)(2,1)S(1)}, bf16[3,4,4,2,80,25...) custom-call(s32[3]{0:T(128)S(1)} %add_convert_fusion.flags, bf16[2560,1024]{1,0:T(8,128)(2,1)} %bitcast.62, ...), custom_call_target="tpu_custom_call" | custom-call | tf_op jit(solution)/shard_map/pallas_call | solution.py:286
  181.2 4.9 %fusion.44 = (bf16[1,4,4,2,80,256]{5,4,3,2,1,0:T(8,128)(2,1)S(1)}, bf16[1,4,4,2,80,256]{5,4,3,2,1,0:T(8,128)(2,1)}, bf16[1,4,4,2,80,256]{5,4,3,2,1,0:T(8,128)(2,1)}) fusion(bf16[3,4,4,2,80,256]{5,4,3,2,1,0:T(8,128)(2,1)} %get-tuple-element.11), kind=kLoop, calls=%fused_computation.72 | loop fusion | bytes 7864320 | tf_op jit(solution)/shard_map/slice | solution.py:462
  186.0 0.8 fusion.46
  186.9 1.6 fusion.45
  188.5 0.9 fusion.12
  189.4 7.0 %fusion.11 = f32[512,2560]{1,0:T(8,128)} fusion(bf16[2560,256]{1,0:T(8,128)(2,1)} %bitcast.65, bf16[512,2560]{1,0:T(8,128)(2,1)S(1)} %bitcast.58, bf16[2560,256]{1,0:T(8,128)(2,1)} %bitcast.66, f32[512,256]{1,0:T(8,128)} %fusion.45), kind=kOutput, calls=%fused_computation.16 | convolution fusion | flops 1342963712 | bytes 11010048 | tf_op jit(solution)/shard_map/dot_general | solution.py:464
  196.4 0.0 all-to-all-done
  196.4 2.3 all_to_all.18
  198.7 4.3 %fusion.39 = f32[128,1024]{1,0:T(8,128)} fusion(bf16[128,2560]{1,0:T(8,128)(2,1)} %all_to_all.18, bf16[1,2560,1024]{2,1,0:T(8,128)(2,1)} %param.16), kind=kOutput, calls=%fused_computation.67 | convolution fusion | flops 671088640 | bytes 6422528 | tf_op jit(solution)/shard_map/dot_general | solution.py:414
  203.1 6.9 %fusion.3 = bf16[128,2560]{1,0:T(8,128)(2,1)} fusion(bf16[1,1024,2560]{2,1,0:T(8,128)(2,1)} %param.18, bf16[128,2560]{1,0:T(8,128)(2,1)} %all_to_all.18, f32[128,1024]{1,0:T(8,128)} %fusion.39, bf16[1,2560,1024]{2,1,0:T(8,128)(2,1)} %param.17), kind=kOutput, calls=%fused_computation.7 | convolution fusion | flops 1343291392 | bytes 12320768 | tf_op jit(solution)/shard_map/dot_general | solution.py:414
  210.0 2.3 all_to_all.19
  212.3 6.2 %all-to-all-start.1 = ((bf16[32,4,2560]{2,1,0:T(4,128)(2,1)}), bf16[32,4,2560]{2,1,0:T(4,128)(2,1)}, u32[]{:S(2)}, u32[]{:S(2)}) async-start(bf16[32,4,2560]{2,1,0:T(4,128)(2,1)} %all_to_all.19), calls=%async_computation.1 | async-start | bytes 1310720 | tf_op jit(solution)/shard_map/all_to_all | solution.py:445
  218.5 8.4 %convolution_add_fusion = f32[512,2560]{1,0:T(8,128)} fusion(f32[512,2560]{1,0:T(8,128)} %fusion.11, bf16[256,2560]{1,0:T(8,128)(2,1)} %bitcast.61, bf16[512,2560]{1,0:T(8,128)(2,1)S(1)} %bitcast.59, bf16[2560,256]{1,0:T(8,128)(2,1)} %copy-done.1, f32[512,256]{1,0:T(8,128)S(1)} %fusion.46, f32[512]{0:T(512)S(1)} %get-tuple-element.19), kind=kOutput, calls=%fused_computation.4 | convolution fusion | flops 1344405504 | bytes 16254976 | tf_op jit(solution)/shard_map/dot_general | solution.py:414
  226.9 7.5 %reshape.163 = f32[4,128,2,2,640]{4,3,2,1,0:T(2,128)} reshape(f32[512,2560]{1,0:T(8,128)} %convolution_add_fusion) | data formatting | bytes 10485760 | tf_op jit(solution)/shard_map/reshape | solution.py:472
  234.5 0.1 dynamic_slice.3
  234.6 1.5 all_to_all.21
  236.0 0.4 convolution_multiply_fusion
  236.4 0.9 mul.88
  237.3 0.1 copy.18
  237.4 3.2 %fusion.6 = bf16[4,2,2,16,8,640]{5,4,3,2,1,0:T(8,128)(2,1)S(1)} fusion(f32[4,128,2,2,640]{4,3,2,1,0:T(2,128)} %reshape.163, f32[128,2,2,640]{3,0,2,1:T(8,128)S(1)} %copy.18, f32[4]{0:T(128)S(1)} %compare_convert_fusion), kind=kLoop, calls=%fused_computation.8 | loop fusion | flops 3932160 | bytes 9175056
  240.6 0.2 copy.21
  240.9 34.5 %shard_map.110 = f32[128,640]{1,0:T(8,128)S(1)} custom-call(bf16[4,2,128,1280]{3,2,1,0:T(8,128)(2,1)S(1)} %bitcast.60), custom_call_target="tpu_custom_call" | custom-call | tf_op jit(solution)/shard_map/pallas_call | solution.py:391
  275.4 0.8 multiply_convert_fusion
  (23 shorter events, 0.1 us)
Async XLA Ops:
  0.0 188.5 %copy-start = (bf16[2560,32]{0,1:T(8,128)(2,1)S(1)}, bf16[2560,32]{0,1:T(8,128)(2,1)}, u32[]{:S(2)}) copy-start(bf16[2560,32]{0,1:T(8,128)(2,1)} %param.15) | copy-start | bytes 491524
  0.0 23.1 %copy-start.7 = (s32[128,1]{0,1:T(1,128)S(1)}, s32[128,1]{0,1:T(1,128)}, u32[]{:S(2)}) copy-start(s32[128,1]{0,1:T(1,128)} %param.12) | copy-start | bytes 1540
  0.0 34.3 %copy-start.4 = (bf16[1024,80]{0,1:T(8,128)(2,1)S(1)}, bf16[1024,80]{0,1:T(8,128)(2,1)}, u32[]{:S(2)}) copy-start(bf16[1024,80]{0,1:T(8,128)(2,1)} %param.21) | copy-start | bytes 491524
  0.0 34.3 %copy-start.6 = (bf16[80,1024]{1,0:T(8,128)(2,1)S(1)}, bf16[80,1024]{1,0:T(8,128)(2,1)}, u32[]{:S(2)}) copy-start(bf16[80,1024]{1,0:T(8,128)(2,1)} %param.19) | copy-start | bytes 491524
  0.0 34.3 %copy-start.5 = (bf16[80,1024]{1,0:T(8,128)(2,1)S(1)}, bf16[80,1024]{1,0:T(8,128)(2,1)}, u32[]{:S(2)}) copy-start(bf16[80,1024]{1,0:T(8,128)(2,1)} %param.20) | copy-start | bytes 491524
  13.5 20.9 %copy-start.3 = (bf16[128,640]{1,0:T(8,128)(2,1)S(1)}, bf16[128,640]{1,0:T(8,128)(2,1)}, u32[]{:S(2)}) copy-start(bf16[128,640]{1,0:T(8,128)(2,1)} %tok.1) | copy-start | bytes 491524
  14.8 181.6 %all-to-all-start = ((bf16[32,4,2560]{2,1,0:T(4,128)(2,1)}), bf16[32,4,2560]{2,1,0:T(4,128)(2,1)}, u32[]{:S(2)}, u32[]{:S(2)}) async-start(bf16[32,4,2560]{2,1,0:T(4,128)(2,1)} %all_to_all.16), calls=%async_computation | async-start | bytes 1310720 | tf_op jit(solution)/shard_map/all_to_all | solution.py:442
  181.1 4.9 %copy-start.1 = (bf16[2560,256]{1,0:T(8,128)(2,1)}, bf16[2560,256]{1,0:T(8,128)(2,1)S(1)}, u32[]{:S(2)}) copy-start(bf16[2560,256]{1,0:T(8,128)(2,1)S(1)} %get-tuple-element.13) | copy-start | bytes 3932164
  181.1 4.9 %copy-start.2 = (bf16[4,2,32,2560]{3,2,1,0:T(8,128)(2,1)}, bf16[4,2,32,2560]{3,2,1,0:T(8,128)(2,1)S(1)}, u32[]{:S(2)}) copy-start(bf16[4,2,32,2560]{3,2,1,0:T(8,128)(2,1)S(1)} %get-tuple-element.14) | copy-start | bytes 3932164
  212.3 22.3 %all-to-all-start.1 = ((bf16[32,4,2560]{2,1,0:T(4,128)(2,1)}), bf16[32,4,2560]{2,1,0:T(4,128)(2,1)}, u32[]{:S(2)}, u32[]{:S(2)}) async-start(bf16[32,4,2560]{2,1,0:T(4,128)(2,1)} %all_to_all.19), calls=%async_computation.1 | async-start | bytes 1310720 | tf_op jit(solution)/shard_map/all_to_all | solution.py:445
  226.9 7.5 %copy-start.8 = (s32[128]{0:T(128)S(1)}, s32[128]{0:T(128)}, u32[]{:S(2)}) copy-start(s32[128]{0:T(128)} %param.13) | copy-start | bytes 1540

commit v2 on v0

v2 whole, which is shorter than its diff:
```python
import jax
import jax.numpy as jnp
from jax import lax
from jax.experimental import pallas as pl
from jax.experimental.pallas import tpu as pltpu
from jax.sharding import PartitionSpec as P

MESH = pl.DeviceIdType.MESH
NX, NY, NZ, NT, CAP = 4, 4, 2, 4, 4


def coords():
    e = lax.axis_index("expert")
    return lax.div(e, NY * NZ), lax.rem(lax.div(e, NZ), NY), lax.rem(e, NZ)


def group_of(x, y, z):
    return (x * NY + y) * NZ + z


def turn(i, n=4):
    return lax.rem(i + 2 * n, n)


class Copies:
    def __init__(self, send, recv, local):
        self.send, self.recv, self.local = send, recv, local
        self.sent, self.kept = 0, 0
        self.started = []

    def remote(self, src, dst, device):
        c = pltpu.make_async_remote_copy(
            src_ref=src,
            dst_ref=dst,
            send_sem=self.send.at[self.sent],
            recv_sem=self.recv.at[self.sent],
            device_id=device,
            device_id_type=MESH,
        )
        self.sent += 1
        c.start()
        self.started.append(c)
        return c

    def here(self, src, dst):
        c = pltpu.make_async_copy(src, dst, self.local.at[self.kept])
        self.kept += 1
        c.start()
        return c


def choose(flag, rows, step, mine, into):
    def body(i, carry):
        at = pl.ds(pl.multiple_of(i * step, step), step)
        into[at] = jnp.where(flag == 1, mine(at), into[at])
        return carry

    lax.fori_loop(0, rows // step, body, 0)


def dot(a, b):
    return jnp.dot(a, b, preferred_element_type=jnp.float32)


def silu(v):
    return v / (1.0 + jnp.exp(-v))


def layer_kernel(
    scalars, tok, slot, mask, router, gate, up, down, sh_own,
    out,
    own_g, own_u, own_d, xg, xu, yg, yu, yd, xd, hg, hu, hd, sh, tk, coefs,
    pack1, got1, pack2, got2, rows_in, home_g, home_u, home_hid,
    acc_g, acc_u, sh_hid, hot_hid, psum, to_core, from_core, mid, from_x, half, from_z,
    w_cols, target_cols,
    send, recv, local, a2a_send, a2a_recv,
):
    x, y, z = coords()
    e = lax.axis_index("expert")
    groups = lax.axis_size("expert")
    t = lax.axis_index("tensor")
    core, z_hi = lax.rem(t, 2), lax.div(t, 2)
    cp = Copies(send, recv, local)
    rows, cols = xg.shape[2], xg.shape[3]
    n, quarter = tok.shape
    bf, f32 = jnp.bfloat16, jnp.float32
    parts = ((0, rows * 3 // 5), (rows * 3 // 5, rows * 2 // 5))

    def at(dx=0, dy=0, dz=0):
        return {"expert": group_of(turn(x + dx), turn(y + dy), turn(z + dz, 2)), "tensor": t}

    other_t = z_hi * 2 + (1 - core)
    across_t = (1 - z_hi) * 2 + core
    other = {"expert": e, "tensor": other_t}
    across = {"expert": e, "tensor": across_t}

    def of_quarter(i):
        return pl.ds(pl.multiple_of(i * quarter, quarter), quarter)

    barrier = pltpu.get_barrier_semaphore()

    def greet(k, carry):
        d = {"expert": lax.rem(e + k, groups), "tensor": t}
        pl.semaphore_signal(barrier, inc=1, device_id=d, device_id_type=MESH)
        return carry

    lax.fori_loop(1, groups, greet, 0)
    for d in (other, across):
        pl.semaphore_signal(barrier, inc=1, device_id=d, device_id_type=MESH)
    pl.semaphore_wait(barrier, groups + 1)
    fx, fy, fz, hot = scalars[0], scalars[1], scalars[2], scalars[3]

    streams = ((gate, own_g, xg, yg, hg, 1), (up, own_u, xu, yu, hu, -1))

    def block(sign, j):
        return turn(y - sign * (1 + j))

    x_copy, own_copy, y_copy, z_copy = {}, {}, {}, {}

    def x_first(h, js):
        off, r = parts[h]
        for j in js:
            for s, (w, _, xb, _, _, sign) in enumerate(streams):
                lanes = pl.ds(pl.multiple_of(turn(x - sign) * cols, cols), cols)
                src = w.at[pl.ds(pl.multiple_of(block(sign, j) * rows + off, 128), r), lanes]
                x_copy[h, s, j, 0] = cp.remote(src, xb.at[j, 0, pl.ds(off, r)], at(sign))

    def own_load(j):
        for s, (w, own, _, _, _, sign) in enumerate(streams):
            src = w.at[pl.ds(pl.multiple_of(block(sign, j) * rows, rows), rows), :]
            own_copy[s, j] = cp.here(src, own.at[j])

    def x_step(h, j, step):
        off, r = parts[h]
        for s, (_, own, xb, _, _, sign) in enumerate(streams):
            x_copy[h, s, j, step].wait_recv()
            if h == 0 and step == 0:
                own_copy[s, j].wait()
            lanes = pl.ds(pl.multiple_of(turn(x - sign * (2 + step)) * cols, cols), cols)
            mine = own.at[j, pl.ds(off, r)]
            into = xb.at[j, step, pl.ds(off, r)]
            choose(fx, r, 128, lambda a, mine=mine, lanes=lanes: mine[a, lanes], into)
            if step < 2:
                nxt = xb.at[j, step + 1, pl.ds(off, r)]
                x_copy[h, s, j, step + 1] = cp.remote(into, nxt, at(sign))

    def y_step(h, j):
        off, r = parts[h]
        for s, (_, _, xb, yb, hb, sign) in enumerate(streams):
            mine = xb.at[j, 2, pl.ds(off, r)]
            if j == 0:
                y_copy[h, s, 0] = cp.remote(mine, yb.at[0, pl.ds(off, r)], at(0, sign))
                continue
            into = yb.at[j - 1, pl.ds(off, r)]
            y_copy[h, s, j - 1].wait_recv()
            choose(fy, r, 128, lambda a, mine=mine: mine[a], into)
            if j < 3:
                y_copy[h, s, j] = cp.remote(into, yb.at[j, pl.ds(off, r)], at(0, sign))
            else:
                z_copy[h, s] = cp.remote(into, hot_rows(hb, h, y), at(0, 0, 1))

    def hot_rows(ref, h, v):
        off, r = parts[h]
        return ref.at[pl.ds(pl.multiple_of(v * rows + off, 128), r)]

    near, far2 = {}, {}

    def spread_y(h):
        off, r = parts[h]
        for s, (_, _, _, yb, hb, sign) in enumerate(streams):
            into = hot_rows(hb, h, y)
            mine = yb.at[2, pl.ds(off, r)]
            z_copy[h, s].wait_recv()
            choose(fz, r, 128, lambda a, mine=mine: mine[a], into)
            near[h, s] = [cp.remote(into, into, at(0, d)) for d in (sign, -sign)]

    def forward_y(h):
        for s, (_, _, _, _, hb, sign) in enumerate(streams):
            near[h, s][0].wait_recv()
            a = hot_rows(hb, h, turn(y - sign))
            far2[h, s] = cp.remote(a, a, at(0, sign))

    def hot_arrived(h):
        for s in (0, 1):
            near[h, s][1].wait_recv()
            far2[h, s].wait_recv()

    d_copy, dx_copy = {}, {}

    def d_first():
        for r, sign in ((0, 1), (1, -1)):
            d_copy[r, 0] = cp.remote(down.at[:, turn(y - sign), r], yd.at[r, 0], at(0, sign))

    def d_step(step):
        for r, sign in ((0, 1), (1, -1)):
            d_copy[r, step].wait_recv()
            yp = turn(y - sign * (2 + step))
            choose(fy, NX, 1, lambda i, yp=yp, r=r: own_d[i, yp, r], yd.at[r, step])
            if step < 2:
                d_copy[r, step + 1] = cp.remote(yd.at[r, step], yd.at[r, step + 1], at(0, sign))

    def dx_step(step):
        for r, sign in ((0, 1), (1, -1)):
            if step == 0:
                dx_copy[r, 0] = cp.remote(yd.at[r, 2, turn(x - sign)], xd.at[r, 0], at(sign))
                continue
            dx_copy[r, step - 1].wait_recv()
            xp = turn(x - sign * (1 + step))
            choose(
                fx, xd.shape[2], 16, lambda i, xp=xp, r=r: yd[r, 2, xp, i], xd.at[r, step - 1]
            )
            if step < 3:
                dx_copy[r, step] = cp.remote(xd.at[r, step - 1], xd.at[r, step], at(sign))

    def exchange(src, dst, base):
        def go(k, carry):
            to = lax.rem(e + k, groups)
            pltpu.make_async_remote_copy(
                src_ref=src.at[to], dst_ref=dst.at[e],
                send_sem=a2a_send.at[base + k], recv_sem=a2a_recv.at[base + k],
                device_id={"expert": to, "tensor": t}, device_id_type=MESH,
            ).start()
            return carry

        lax.fori_loop(1, groups, go, 0)
        return cp.here(src.at[e], dst.at[e])

    def exchanged(src, dst, base, sends):
        def done(k, carry):
            to = lax.rem(e + k, groups)
            frm = lax.rem(e + groups - k, groups)
            c = pltpu.make_async_remote_copy(
                src_ref=src.at[to], dst_ref=dst.at[frm],
                send_sem=a2a_send.at[base + k], recv_sem=a2a_recv.at[base + k],
                device_id={"expert": to, "tensor": t}, device_id_type=MESH,
            )
            if sends:
                c.wait_send()
            else:
                c.wait_recv()
            return carry

        lax.fori_loop(1, groups, done, 0)

    def iota(shape, dim):
        return lax.broadcasted_iota(jnp.int32, shape, dim)

    def as_row(col):
        eye = iota((n, n), 0) == iota((n, n), 1)
        return jnp.sum(jnp.where(eye, col, 0.0), axis=0, keepdims=True)

    def as_col(row):
        eye = iota((n, n), 0) == iota((n, n), 1)
        return jnp.sum(jnp.where(eye, row, 0.0), axis=1, keepdims=True)

    blocks_at_once = n // 16

    def packed(c, q, key):
        r = iota((n, n), 0) + c * n
        of = (r // 16) * 4 + r % 4
        return ((of.astype(f32) == key) & ((r // 4) % 4 == q)).astype(bf)

    def unpacked(q, key):
        r = iota((n, 4 * n), 1)
        of = (r // 16) * 4 + r % 4
        return ((of.astype(f32) == key) & ((r // 4) % 4 == q)).astype(bf)

    mine = of_quarter(t)
    t_peer = [cp.remote(tok, tk.at[0, :, mine], d) for d in (other, across)]
    x_first(0, (0, 1))
    d_first()
    t_own = cp.here(tok, tk.at[0, :, mine])
    t_x = [cp.remote(tok, tk.at[(4 - d) % 4, :, mine], at(d)) for d in (1, -1, 2)]

    def sh_piece(xp):
        return sh_own.at[:, :, pl.ds(pl.multiple_of(xp * cols, cols), cols)]

    s_x = [cp.remote(sh_piece(turn(x + d)), sh.at[:, x, y, z], at(d)) for d in (1, -1, 2)]
    s_own = cp.here(sh_piece(x), sh.at[:, x, y, z])
    x_first(0, (2, 3))
    own_load(0)
    own_d_copy = cp.here(down, own_d)
    for j in (1, 2, 3):
        own_load(j)

    ids = slot[...]
    spare = (ids & 1) == 1
    expert = ids >> 1
    ids_f = ids.astype(f32)
    same = jnp.where(
        (ids_f == as_row(ids_f)) & (iota((n, n), 1) < iota((n, n), 0)), 1.0, 0.0
    )
    position = jnp.sum(same, axis=1, keepdims=True)
    target = jnp.where(spare, -1.0, expert.astype(f32) * CAP + position)
    target_cols[...] = jnp.broadcast_to(target, target_cols.shape)

    t_own.wait()
    t_peer[1].wait_recv()
    a = tk.at[0, :, of_quarter(across_t)]
    t_fwd = cp.remote(a, a, other)
    t_peer[0].wait_recv()
    t_fwd.wait_recv()
    target_row = as_row(target)
    for c in range(4):
        acc = jnp.zeros((n, quarter), f32)
        for q in range(4):
            acc += dot(packed(c, q, target_row), tk[0, :, q * quarter : (q + 1) * quarter])
        pack1[c * blocks_at_once : (c + 1) * blocks_at_once] = acc.astype(bf).reshape(
            blocks_at_once, 16, quarter
        )
    own1 = exchange(pack1, got1, 0)
    logits = dot(tk[0], router[...])
    chosen = jnp.where(spare, hot, expert) == iota(logits.shape, 1)
    w = jax.nn.sigmoid(jnp.sum(jnp.where(chosen, logits, 0.0), axis=1, keepdims=True))
    w_cols[...] = jnp.broadcast_to(w, w_cols.shape)
    coefs[0] = jnp.broadcast_to(as_row(jnp.where(spare, w, 0.0)), coefs.shape[1:])
    c_x = [cp.remote(coefs.at[0], coefs.at[(4 - d) % 4], at(d)) for d in (1, -1, 2)]

    def unpack_rows():
        exchanged(pack1, got1, 0, False)
        own1.wait()
        flat = got1[...].reshape(4 * n, quarter)
        key = iota((n, 1), 0).astype(f32)
        for q in range(4):
            rows_in[:, q * quarter : (q + 1) * quarter] = dot(unpacked(q, key), flat).astype(bf)

    def home_in(j):
        for acc, own, sign in ((home_g, own_g, 1), (home_u, own_u, -1)):
            a = rows_in[:, pl.ds(pl.multiple_of(block(sign, j) * rows, rows), rows)]
            v = dot(a, own[j])
            acc[...] = v if j == 0 else acc[...] + v

    def home_mid():
        home_hid[...] = (silu(home_g[...]) * home_u[...]).astype(bf)

    def home_out(q):
        lanes = slice(q * quarter, (q + 1) * quarter)
        v = jnp.zeros((n, quarter), f32)
        for i in range(NX):
            wd = own_d[i, :, :, :, lanes].reshape(cols, quarter)
            v += dot(home_hid[:, i * cols : (i + 1) * cols], wd)
        acc_rows = v.astype(bf)
        row = iota((1, n), 1).astype(f32)
        for c in range(4):
            a = slice(c * blocks_at_once, (c + 1) * blocks_at_once)
            p = dot(packed(c, q, row), acc_rows).astype(bf).reshape(blocks_at_once, 16, quarter)
            pack2[a] = p if q == 0 else pack2[a] + p

    def home_back():
        exchanged(pack2, got2, groups, False)
        own2.wait()
        flat = got2[...].reshape(4 * n, quarter)
        key = target_cols[:, 0:1]
        for q in range(4):
            back = dot(unpacked(q, key), flat)
            psum[0, q] = psum[0, q] + w_cols[:, 0:1] * back

    def quad_in(lanes, w_gate, w_up, first):
        a = tk[:, :, lanes].reshape(NX * n, -1)
        for acc, wt in ((acc_g, w_gate), (acc_u, w_up)):
            v = dot(a, wt)
            acc[...] = v if first else acc[...] + v

    def shared_in(k):
        quad_in(
            slice(k * rows, (k + 1) * rows),
            sh[0, k].reshape(rows, cols), sh[1, k].reshape(rows, cols), k == 0,
        )

    def shared_mid():
        sh_hid[...] = (silu(acc_g[...]) * acc_u[...]).astype(bf)

    def shared_out(q):
        wt = sh[2, q].reshape(quarter, cols)
        v = lax.dot_general(
            sh_hid[...], wt, (((1,), (1,)), ((), ())), preferred_element_type=f32
        )
        psum[:, q] = v.reshape(NX, n, quarter)

    def hot_in(h, k):
        off, r = parts[h]
        lanes = slice(k * rows + off, k * rows + off + r)
        quad_in(lanes, hg[lanes], hu[lanes], h == 0 and k == 0)

    x_step(0, 0, 0)
    x_step(0, 1, 0)
    for c in t_x:
        c.wait_recv()
    t_t = [cp.remote(tk.at[1:4, :, mine], tk.at[1:4, :, mine], d) for d in (other, across)]
    for c in s_x:
        c.wait_recv()
    s_own.wait()
    s_y = [cp.remote(sh.at[:, :, y, z], sh.at[:, :, y, z], at(0, d)) for d in (1, -1)]
    s_z = [cp.remote(sh.at[:, :, y, z], sh.at[:, :, y, z], at(0, 0, 1))]
    x_step(0, 2, 0)
    x_step(0, 3, 0)
    own_d_copy.wait()
    d_step(0)
    x_step(0, 0, 1)
    x_step(0, 1, 1)
    t_t[1].wait_recv()
    a = tk.at[1:4, :, of_quarter(across_t)]
    t_fwd2 = cp.remote(a, a, other)
    unpack_rows()
    x_step(0, 2, 1)
    x_step(0, 3, 1)
    x_first(1, (0, 1, 2, 3))
    home_in(0)
    for c in s_y:
        c.wait_recv()
    lo, hi, opp = turn(y - 1), turn(y + 1), turn(y + 2)
    s_y2 = [
        cp.remote(sh.at[:, 0:2, lo, z], sh.at[:, 0:2, lo, z], at(0, 1)),
        cp.remote(sh.at[:, 2:4, hi, z], sh.at[:, 2:4, hi, z], at(0, -1)),
    ]
    s_z += [cp.remote(sh.at[:, :, v, z], sh.at[:, :, v, z], at(0, 0, 1)) for v in (lo, hi)]
    d_step(1)
    home_in(1)
    x_step(0, 0, 2)
    y_step(0, 0)
    home_in(2)
    x_step(0, 1, 2)
    y_step(0, 1)
    home_in(3)
    home_mid()
    x_step(0, 2, 2)
    y_step(0, 2)
    home_out(0)
    home_out(1)
    x_step(0, 3, 2)
    y_step(0, 3)
    d_step(2)
    dx_step(0)
    home_out(2)
    home_out(3)
    own2 = exchange(pack2, got2, groups)
    for c in s_y2:
        c.wait_recv()
    s_z.append(cp.remote(sh.at[:, :, opp, z], sh.at[:, :, opp, z], at(0, 0, 1)))
    x_step(1, 0, 0)
    x_step(1, 1, 0)
    spread_y(0)
    dx_step(1)
    x_step(1, 2, 0)
    x_step(1, 3, 0)
    dx_step(2)
    x_step(1, 0, 1)
    x_step(1, 1, 1)
    dx_step(3)
    d_z = [cp.remote(xd.at[r, 2], hd.at[y, r], at(0, 0, 1)) for r in (0, 1)]
    forward_y(0)
    x_step(1, 2, 1)
    x_step(1, 3, 1)
    for c in t_t[:1] + [t_fwd2] + s_z:
        c.wait_recv()
    d_y = []
    for r in (0, 1):
        d_z[r].wait_recv()
        choose(fz, xd.shape[2], 16, lambda i, r=r: xd[r, 2, i], hd.at[y, r])
        d_y.append([cp.remote(hd.at[y, r], hd.at[y, r], at(0, d)) for d in (1, -1)])
    shared_in(0)
    shared_in(1)
    x_step(1, 0, 2)
    y_step(1, 0)
    shared_in(2)
    shared_in(3)
    shared_mid()
    x_step(1, 1, 2)
    y_step(1, 1)
    d_y[0][0].wait_recv()
    d_y[1][1].wait_recv()
    d_y2 = [
        cp.remote(hd.at[lo, 0], hd.at[lo, 0], at(0, 1)),
        cp.remote(hd.at[hi, 1], hd.at[hi, 1], at(0, -1)),
    ]
    shared_out(0)
    shared_out(1)
    x_step(1, 2, 2)
    y_step(1, 2)
    shared_out(2)
    shared_out(3)
    x_step(1, 3, 2)
    y_step(1, 3)
    home_back()
    spread_y(1)
    hot_arrived(0)
    for k in range(4):
        hot_in(0, k)
    forward_y(1)
    for c in c_x:
        c.wait_recv()
    hot_arrived(1)
    for k in range(4):
        hot_in(1, k)
    d_y[0][1].wait_recv()
    d_y[1][0].wait_recv()
    for c in d_y2:
        c.wait_recv()
    for d in range(NX):
        a = slice(d * n, (d + 1) * n)
        hot_hid[a] = (
            silu(acc_g[a]) * acc_u[a] * as_col(coefs[d, 0:1])
        ).astype(bf)

    order = (2, 1, 3, 0)
    to_c = {}
    for d in order:
        for q in range(4):
            lanes = slice(q * quarter, (q + 1) * quarter)
            wd = hd[:, :, :, lanes].reshape(cols, quarter)
            psum[d, q] = psum[d, q] + dot(hot_hid[d * n : (d + 1) * n], wd)
        to_core[d, :, 0:quarter] = psum[d, 1 - core].astype(bf)
        to_core[d, :, quarter:] = psum[d, 3 - core].astype(bf)
        to_c[d] = cp.remote(to_core.at[d], from_core.at[d], other)
    to_x = []
    for d in order:
        to_c[d].wait_recv()
        if d:
            for i, q in enumerate((core, 2 + core)):
                lanes = slice(i * quarter, (i + 1) * quarter)
                mid[d - 1, :, lanes] = (psum[d, q] + from_core[d, :, lanes].astype(f32)).astype(bf)
            to_x.append(cp.remote(mid.at[d - 1], from_x.at[d - 1], at(d)))
    for c in to_x:
        c.wait_recv()

    def total(side):
        lanes = of_quarter(side)
        v = psum[0, 2 * side + core] + from_core[0, :, lanes].astype(f32)
        for i in range(3):
            v += from_x[i, :, lanes].astype(f32)
        return v

    half[...] = total(1 - z_hi).astype(bf)
    last = cp.remote(half, from_z, across)
    own_total = total(z_hi)
    last.wait_recv()
    out[...] = (mask[...].astype(f32) * (own_total + from_z[...].astype(f32))).astype(out.dtype)
    for c in cp.started:
        c.wait_send()
    exchanged(pack1, got1, 0, True)
    exchanged(pack2, got2, groups, True)


def local(
    tokens, slot, mask, hot_group, router_weight,
    exp_gate, exp_up, exp_down, sh_gate, sh_up, sh_down,
):
    bf, f32 = jnp.bfloat16, jnp.float32
    x, y, z = coords()
    hot = hot_group[0]
    hx, hy, hz = hot // (NY * NZ), (hot // NZ) % NY, hot % NZ
    scalars = jnp.stack(
        [(hx == x).astype(jnp.int32), (hy == y).astype(jnp.int32), (hz == z).astype(jnp.int32), hot]
    )
    n, quarter = tokens.shape
    d, h = exp_gate.shape[1:]
    rows, cols = d // NY, h // NX
    part = cols // (2 * NY)
    groups = NX * NY * NZ
    sh_own = jnp.stack([sh_gate, sh_up, sh_down.T])
    any_spec = pl.BlockSpec(memory_space=pl.ANY)
    vmem = pl.BlockSpec(memory_space=pltpu.VMEM)
    blocks = pltpu.VMEM((groups, 16, quarter), bf)
    return pl.pallas_call(
        layer_kernel,
        out_shape=jax.ShapeDtypeStruct((n, quarter), bf),
        in_specs=[pl.BlockSpec(memory_space=pltpu.SMEM), any_spec, vmem, vmem, vmem]
        + [any_spec] * 4,
        out_specs=vmem,
        scratch_shapes=[
            pltpu.VMEM((NY, rows, h), bf),
            pltpu.VMEM((NY, rows, h), bf),
            pltpu.VMEM((NX, NY, 2, part, d), bf),
            pltpu.VMEM((NY, 3, rows, cols), bf),
            pltpu.VMEM((NY, 3, rows, cols), bf),
            pltpu.VMEM((3, rows, cols), bf),
            pltpu.VMEM((3, rows, cols), bf),
            pltpu.VMEM((2, 3, NX, part, d), bf),
            pltpu.VMEM((2, 3, part, d), bf),
            pltpu.VMEM((d, cols), bf),
            pltpu.VMEM((d, cols), bf),
            pltpu.VMEM((NY, 2, part, d), bf),
            pltpu.VMEM((3, NX, NY, NZ, sh_own.shape[1], cols), bf),
            pltpu.VMEM((NX, n, d), bf),
            pltpu.VMEM((NX, 8, n), f32),
            blocks, blocks, blocks, blocks,
            pltpu.VMEM((n, d), bf),
            pltpu.VMEM((n, h), f32),
            pltpu.VMEM((n, h), f32),
            pltpu.VMEM((n, h), bf),
            pltpu.VMEM((NX * n, cols), f32),
            pltpu.VMEM((NX * n, cols), f32),
            pltpu.VMEM((NX * n, cols), bf),
            pltpu.VMEM((NX * n, cols), bf),
            pltpu.VMEM((NX, NT, n, quarter), f32),
            pltpu.VMEM((NX, n, 2 * quarter), bf),
            pltpu.VMEM((NX, n, 2 * quarter), bf),
            pltpu.VMEM((3, n, 2 * quarter), bf),
            pltpu.VMEM((3, n, 2 * quarter), bf),
            pltpu.VMEM((n, quarter), bf),
            pltpu.VMEM((n, quarter), bf),
            pltpu.VMEM((n, 128), f32),
            pltpu.VMEM((n, 128), f32),
            pltpu.SemaphoreType.DMA((140,)),
            pltpu.SemaphoreType.DMA((140,)),
            pltpu.SemaphoreType.DMA((16,)),
            pltpu.SemaphoreType.DMA((2 * groups,)),
            pltpu.SemaphoreType.DMA((2 * groups,)),
        ],
        compiler_params=pltpu.CompilerParams(
            collective_id=0, has_side_effects=True, vmem_limit_bytes=62 * 2**20
        ),
    )(
        scalars, tokens, slot, mask.reshape(n, 1), router_weight,
        exp_gate[0], exp_up[0], exp_down[0].reshape(NX, NY, 2, part, d), sh_own,
    )


def solution(mesh):
    in_specs = (
        P("expert", "tensor"),
        P("expert", None),
        P("expert"),
        P(),
        P(),
        P("expert", None, "tensor"),
        P("expert", None, "tensor"),
        P("expert", "tensor", None),
        P("expert", "tensor"),
        P("expert", "tensor"),
        P("tensor", "expert"),
    )
    out_specs = P("expert", "tensor")
    return jax.shard_map(local, mesh=mesh, in_specs=in_specs, out_specs=out_specs, check_vma=False)
```

time: 1160 us -> 216 us (0.19)
  waiting for transfers between devices: 1020 us -> 0 us
  Pallas kernels: 0 us -> 206 us
  matrix products: 46.1 us -> 0 us
  starting transfers between devices: 19.8 us -> 0 us
  blocking collectives: 19.5 us -> 0 us
  other arithmetic: 18.3 us -> 2.52 us
  between operations: 15.4 us -> 0.72 us
    psum x1 -> x0, waiting for transfers between devices: 963 us -> none  [from_root(): return lax.psum(block, axis)]
    pallas_call x0 -> x1, Pallas kernels: none -> 206 us  [local(): pl.pallas_call(layer_kernel, out_shape=jax.ShapeDtypeStruct((n, quarter),...]
    all_to_all x3 -> x0, waiting for transfers between devices: 54.7 us -> none  [the longest x1 38.9 us: sent_and_summed(): lax.all_to_all(tiles, axis, split_axis=0, concat_axis=0, tiled=True)]
    dot_general x10 -> x0, matrix products: 46.1 us -> none  [the longest x2 11.1 us: expert_ffn(): return jnp.dot(hidden, w_down, preferred_element_type=jnp.float32)]
    all_to_all x3 -> x0, starting transfers between devices: 19.6 us -> none  [the longest x1 9.22 us: local(): lax.all_to_all(outgoing, 'expert', split_axis=0, concat_axis=0, tiled=True)]
    all_gather x1 -> x0, blocking collectives: 19.5 us -> none  [local(): whole = lax.all_gather(tokens, 'tensor', axis=1, tiled=True)]
    select_n x2 -> x0, other arithmetic: 13.9 us -> none  [from_root(): jnp.where(lax.axis_index(axis) == source, block, jnp.zeros_like(block))]
  transfers between devices with their start and end apart: 8 -> 0, of which waited for: 4 -> 0; matrix products, arithmetic and copies ran while one was open for 5% -> 0% of each run, Pallas kernels for 0% -> 0%
where the time goes in v2:
time: 216 us
  Pallas kernels  206 us (95%)
  local copies, waits for them, and re-layouts  6.35 us (3%)
  other arithmetic  2.52 us (1%)
    pallas_call x1, Pallas kernels, local(): pl.pallas_call(layer_kernel, out_shape=jax.ShapeDtypeStruct((n, quarter),...  206 us
    unnamed x3, local copies, waits for them, and re-layouts  4.98 us

profile of v2, /device:TPU:1, one launch (start us, length us, event | category | flops | bytes accessed | tf_op | source)
XLA Modules:
  0.0 215.7 jit_solution(16412820171810179775)
XLA Ops:
  0.7 0.6 pad_add_fusion.scalars
  1.3 1.4 copy.12.slot
  2.7 1.4 copy.13.mask
  4.1 1.9 pad_maximum_fusion.sh_own
  6.0 2.0 copy.14.router
  8.0 206.1 %shard_map.109 = bf16[128,640]{1,0:T(8,128)(2,1)} custom-call(s32[4]{0:T(128)} %pad_add_fusion.scalars, bf16[128,640]{1,0:T(8,128)(2,1)} %tok.1, s32[128,1]{1,0:T(8,128)} %copy.12.slot, s32[128,1]{1,0:T(8,128)} %copy.13.mask, bf16[2560,32]{1,0:T(8,128)(2,1)} %copy.14.router, bf16[2560,1024]{1,0:T(8,128)(2,1)} %bitcast.17, bf16[2560,1024]{1,0:T(8,128)(2,1)} %bitcast.18, ...), custom_call_target="tpu_custom_call" | custom-call | tf_op jit(solution)/shard_map/pallas_call | solution.py:564
  214.1 1.6 copy.17

commit v3 on v2

--- a/solution.py
+++ b/solution.py
@@ -8,6 +8,22 @@
 MESH = pl.DeviceIdType.MESH
 NX, NY, NZ, NT, CAP = 4, 4, 2, 4, 4
 
+PARTS = ((0, 256), (256, 256), (512, 128))
+SPLIT = 384
+SENDS = 240
+ORDER = (
+    "tok0", "df", "own0", "tokx", "sx", "route", "pack", "wts", "tt", "s1", "d0", "xf00", "xf01",
+    "xf03", "unpack", "x000", "hi0", "hi1", "x010", "hi2", "hi3", "x030", "hm", "tf", "ho0", "x001",
+    "ho1", "ho2", "x011", "ho3", "s2", "ex2", "x031", "tq", "x002", "y00", "x012", "d1", "xf10",
+    "xf02", "s3", "x032", "xf11", "x100", "x020", "x110", "y01", "x101", "x021", "x111", "x102",
+    "y10", "xf12", "x022", "d2", "dx0", "x112", "y02", "si0", "x120", "si1", "y11", "si2", "dx1",
+    "y03", "si3", "xf20", "sm", "x121", "so0", "so1", "dx2", "so2", "so3", "hb", "x122", "y12",
+    "sy0", "xf13", "x200", "dx3", "dz0", "xf22", "xf21", "x130", "x201", "fy0", "x220", "x210",
+    "dy1", "x131", "hot0", "x202", "y20", "x221", "x211", "dy2", "xf23", "x132", "y13", "x222",
+    "x212", "y21", "x230", "y22", "x231", "sy1", "x232", "y23", "fy1", "sy2", "hot1", "fy2", "hot2",
+    "end",
+)
+
 
 def coords():
     e = lax.axis_index("expert")
@@ -27,6 +43,7 @@
         self.send, self.recv, self.local = send, recv, local
         self.sent, self.kept = 0, 0
         self.started = []
+        self.waited = set()
 
     def remote(self, src, dst, device):
         c = pltpu.make_async_remote_copy(
@@ -48,6 +65,22 @@
         c.start()
         return c
 
+    def once(self, c, remote):
+        if id(c) not in self.waited:
+            self.waited.add(id(c))
+            if remote:
+                c.wait_recv()
+            else:
+                c.wait()
+
+    def got(self, *copies):
+        for c in copies:
+            self.once(c, True)
+
+    def placed(self, *copies):
+        for c in copies:
+            self.once(c, False)
+
 
 def choose(flag, rows, step, mine, into):
     def body(i, carry):
@@ -67,12 +100,12 @@
 
 
 def layer_kernel(
-    scalars, tok, slot, mask, router, gate, up, down, sh_own,
+    scalars, tok, slot, router, gate, up, down, sh_gate, sh_up, sh_down,
     out,
     own_g, own_u, own_d, xg, xu, yg, yu, yd, xd, hg, hu, hd, sh, tk, coefs,
     pack1, got1, pack2, got2, rows_in, home_g, home_u, home_hid,
-    acc_g, acc_u, sh_hid, hot_hid, psum, to_core, from_core, mid, from_x, half, from_z,
-    w_cols, target_cols,
+    acc_g, acc_u, sh_hid, hot_hid, psum, to_core, from_core, mid, from_x, half, from_z, from_zb, mid_b, from_xb,
+    w_cols, target_cols, expert_cols,
     send, recv, local, a2a_send, a2a_recv,
 ):
     x, y, z = coords()
@@ -84,7 +117,7 @@
     rows, cols = xg.shape[2], xg.shape[3]
     n, quarter = tok.shape
     bf, f32 = jnp.bfloat16, jnp.float32
-    parts = ((0, rows * 3 // 5), (rows * 3 // 5, rows * 2 // 5))
+    parts = PARTS
 
     def at(dx=0, dy=0, dz=0):
         return {"expert": group_of(turn(x + dx), turn(y + dy), turn(z + dz, 2)), "tensor": t}
@@ -134,8 +167,7 @@
         off, r = parts[h]
         for s, (_, own, xb, _, _, sign) in enumerate(streams):
             x_copy[h, s, j, step].wait_recv()
-            if h == 0 and step == 0:
-                own_copy[s, j].wait()
+            cp.placed(own_copy[s, j])
             lanes = pl.ds(pl.multiple_of(turn(x - sign * (2 + step)) * cols, cols), cols)
             mine = own.at[j, pl.ds(off, r)]
             into = xb.at[j, step, pl.ds(off, r)]
@@ -194,6 +226,7 @@
     def d_step(step):
         for r, sign in ((0, 1), (1, -1)):
             d_copy[r, step].wait_recv()
+            cp.placed(c_of["down"])
             yp = turn(y - sign * (2 + step))
             choose(fy, NX, 1, lambda i, yp=yp, r=r: own_d[i, yp, r], yd.at[r, step])
             if step < 2:
@@ -266,59 +299,112 @@
         return ((of.astype(f32) == key) & ((r // 4) % 4 == q)).astype(bf)
 
     mine = of_quarter(t)
-    t_peer = [cp.remote(tok, tk.at[0, :, mine], d) for d in (other, across)]
-    x_first(0, (0, 1))
-    d_first()
-    t_own = cp.here(tok, tk.at[0, :, mine])
-    t_x = [cp.remote(tok, tk.at[(4 - d) % 4, :, mine], at(d)) for d in (1, -1, 2)]
-
-    def sh_piece(xp):
-        return sh_own.at[:, :, pl.ds(pl.multiple_of(xp * cols, cols), cols)]
-
-    s_x = [cp.remote(sh_piece(turn(x + d)), sh.at[:, x, y, z], at(d)) for d in (1, -1, 2)]
-    s_own = cp.here(sh_piece(x), sh.at[:, x, y, z])
-    x_first(0, (2, 3))
-    own_load(0)
-    own_d_copy = cp.here(down, own_d)
-    for j in (1, 2, 3):
-        own_load(j)
-
-    ids = slot[...]
-    spare = (ids & 1) == 1
-    expert = ids >> 1
-    ids_f = ids.astype(f32)
-    same = jnp.where(
-        (ids_f == as_row(ids_f)) & (iota((n, n), 1) < iota((n, n), 0)), 1.0, 0.0
-    )
-    position = jnp.sum(same, axis=1, keepdims=True)
-    target = jnp.where(spare, -1.0, expert.astype(f32) * CAP + position)
-    target_cols[...] = jnp.broadcast_to(target, target_cols.shape)
-
-    t_own.wait()
-    t_peer[1].wait_recv()
-    a = tk.at[0, :, of_quarter(across_t)]
-    t_fwd = cp.remote(a, a, other)
-    t_peer[0].wait_recv()
-    t_fwd.wait_recv()
-    target_row = as_row(target)
-    for c in range(4):
-        acc = jnp.zeros((n, quarter), f32)
-        for q in range(4):
-            acc += dot(packed(c, q, target_row), tk[0, :, q * quarter : (q + 1) * quarter])
-        pack1[c * blocks_at_once : (c + 1) * blocks_at_once] = acc.astype(bf).reshape(
-            blocks_at_once, 16, quarter
+    theirs = of_quarter(across_t)
+    c_of = {}
+
+    def own_tokens():
+        c_of["peer"] = [cp.remote(tok, tk.at[0, :, mine], d) for d in (other, across)]
+        c_of["own"] = cp.here(tok, tk.at[0, :, mine])
+
+    def quad_tokens():
+        c_of["quad"] = [cp.remote(tok, tk.at[(4 - d) % 4, :, mine], at(d)) for d in (2, 1, -1)]
+
+    def quad_across():
+        cp.got(*c_of["quad"])
+        a = tk.at[1:4, :, mine]
+        c_of["quad_peer"] = [cp.remote(a, a, d) for d in (other, across)]
+
+    def quad_relay():
+        cp.got(c_of["quad_peer"][1])
+        a = tk.at[1:4, :, theirs]
+        c_of["quad_relay"] = cp.remote(a, a, other)
+
+    def quad_done():
+        cp.got(c_of["quad_peer"][0], c_of["quad_relay"])
+
+    def own_loads():
+        for j in range(4):
+            own_load(j)
+            if j == 0:
+                c_of["down"] = cp.here(down, own_d)
+
+    sh_refs = (sh_gate, sh_up, sh_down)
+
+    def sh_piece(i, xp):
+        return sh_refs[i].at[:, pl.ds(pl.multiple_of(xp * cols, cols), cols)]
+
+    lo, hi, opp = turn(y - 1), turn(y + 1), turn(y + 2)
+
+    def sh_x():
+        c_of["sh_x"] = [
+            cp.remote(sh_piece(i, turn(x + d)), sh.at[i, x, y, z], at(d))
+            for d in (2, 1, -1)
+            for i in range(3)
+        ]
+        c_of["sh_own"] = [cp.here(sh_piece(i, x), sh.at[i, x, y, z]) for i in range(3)]
+
+    def sh_to(a, device):
+        return cp.remote(a, a, device)
+
+    def sh_1():
+        cp.got(*c_of["sh_x"])
+        cp.placed(*c_of["sh_own"])
+        c_of["sh_y"] = [sh_to(sh.at[:, :, y, z], at(0, d)) for d in (1, -1)]
+        c_of["sh_z"] = [sh_to(sh.at[:, :, y, z], at(0, 0, 1))]
+
+    def sh_2():
+        cp.got(*c_of["sh_y"])
+        c_of["sh_y2"] = [
+            sh_to(sh.at[:, 0:2, lo, z], at(0, 1)), sh_to(sh.at[:, 2:4, hi, z], at(0, -1))
+        ]
+        c_of["sh_z"] += [sh_to(sh.at[:, :, v, z], at(0, 0, 1)) for v in (lo, hi)]
+
+    def sh_3():
+        cp.got(*c_of["sh_y2"])
+        c_of["sh_z"].append(sh_to(sh.at[:, :, opp, z], at(0, 0, 1)))
+
+    def route():
+        ids_row = slot[...].astype(f32)
+        ids_f = as_col(ids_row)
+        ids = ids_f.astype(jnp.int32)
+        same = jnp.where((ids_f == ids_row) & (iota((n, n), 1) < iota((n, n), 0)), 1.0, 0.0)
+        position = jnp.sum(same, axis=1, keepdims=True)
+        spare = (ids & 1) == 1
+        target = jnp.where(spare, -1.0, (ids >> 1).astype(f32) * CAP + position)
+        target_cols[...] = jnp.broadcast_to(target, target_cols.shape)
+        expert = jnp.where(spare, hot, ids >> 1)
+        expert_cols[...] = jnp.broadcast_to(expert, expert_cols.shape)
+        cp.placed(c_of["own"])
+        cp.got(c_of["peer"][1])
+        a = tk.at[0, :, theirs]
+        c_of["relay"] = cp.remote(a, a, other)
+
+    def pack():
+        cp.got(c_of["peer"][0], c_of["relay"])
+        target_row = as_row(target_cols[:, 0:1])
+        for c in range(4):
+            acc = jnp.zeros((n, quarter), f32)
+            for q in range(4):
+                acc += dot(packed(c, q, target_row), tk[0, :, q * quarter : (q + 1) * quarter])
+            pack1[c * blocks_at_once : (c + 1) * blocks_at_once] = acc.astype(bf).reshape(
+                blocks_at_once, 16, quarter
+            )
+        c_of["own1"] = exchange(pack1, got1, 0)
+
+    def weights():
+        logits = lax.dot_general(
+            tk[0], router[...], (((1,), (1,)), ((), ())), preferred_element_type=f32
         )
-    own1 = exchange(pack1, got1, 0)
-    logits = dot(tk[0], router[...])
-    chosen = jnp.where(spare, hot, expert) == iota(logits.shape, 1)
-    w = jax.nn.sigmoid(jnp.sum(jnp.where(chosen, logits, 0.0), axis=1, keepdims=True))
-    w_cols[...] = jnp.broadcast_to(w, w_cols.shape)
-    coefs[0] = jnp.broadcast_to(as_row(jnp.where(spare, w, 0.0)), coefs.shape[1:])
-    c_x = [cp.remote(coefs.at[0], coefs.at[(4 - d) % 4], at(d)) for d in (1, -1, 2)]
+        chosen = expert_cols[:, 0 : logits.shape[1]] == iota(logits.shape, 1)
+        w = jax.nn.sigmoid(jnp.sum(jnp.where(chosen, logits, 0.0), axis=1, keepdims=True))
+        w_cols[...] = jnp.broadcast_to(w, w_cols.shape)
+        coef = jnp.where(target_cols[:, 0:1] < 0, w, 0.0)
+        coefs[0] = jnp.broadcast_to(as_row(coef), coefs.shape[1:])
+        c_of["coef"] = [cp.remote(coefs.at[0], coefs.at[(4 - d) % 4], at(d)) for d in (2, 1, -1)]
 
     def unpack_rows():
         exchanged(pack1, got1, 0, False)
-        own1.wait()
+        cp.placed(c_of["own1"])
         flat = got1[...].reshape(4 * n, quarter)
         key = iota((n, 1), 0).astype(f32)
         for q in range(4):
@@ -326,6 +412,7 @@
 
     def home_in(j):
         for acc, own, sign in ((home_g, own_g, 1), (home_u, own_u, -1)):
+            cp.placed(own_copy[0 if sign == 1 else 1, j])
             a = rows_in[:, pl.ds(pl.multiple_of(block(sign, j) * rows, rows), rows)]
             v = dot(a, own[j])
             acc[...] = v if j == 0 else acc[...] + v
@@ -334,6 +421,7 @@
         home_hid[...] = (silu(home_g[...]) * home_u[...]).astype(bf)
 
     def home_out(q):
+        cp.placed(c_of["down"])
         lanes = slice(q * quarter, (q + 1) * quarter)
         v = jnp.zeros((n, quarter), f32)
         for i in range(NX):
@@ -348,7 +436,7 @@
 
     def home_back():
         exchanged(pack2, got2, groups, False)
-        own2.wait()
+        cp.placed(c_of["own2"])
         flat = got2[...].reshape(4 * n, quarter)
         key = target_cols[:, 0:1]
         for q in range(4):
@@ -382,159 +470,109 @@
         lanes = slice(k * rows + off, k * rows + off + r)
         quad_in(lanes, hg[lanes], hu[lanes], h == 0 and k == 0)
 
-    x_step(0, 0, 0)
-    x_step(0, 1, 0)
-    for c in t_x:
-        c.wait_recv()
-    t_t = [cp.remote(tk.at[1:4, :, mine], tk.at[1:4, :, mine], d) for d in (other, across)]
-    for c in s_x:
-        c.wait_recv()
-    s_own.wait()
-    s_y = [cp.remote(sh.at[:, :, y, z], sh.at[:, :, y, z], at(0, d)) for d in (1, -1)]
-    s_z = [cp.remote(sh.at[:, :, y, z], sh.at[:, :, y, z], at(0, 0, 1))]
-    x_step(0, 2, 0)
-    x_step(0, 3, 0)
-    own_d_copy.wait()
-    d_step(0)
-    x_step(0, 0, 1)
-    x_step(0, 1, 1)
-    t_t[1].wait_recv()
-    a = tk.at[1:4, :, of_quarter(across_t)]
-    t_fwd2 = cp.remote(a, a, other)
-    unpack_rows()
-    x_step(0, 2, 1)
-    x_step(0, 3, 1)
-    x_first(1, (0, 1, 2, 3))
-    home_in(0)
-    for c in s_y:
-        c.wait_recv()
-    lo, hi, opp = turn(y - 1), turn(y + 1), turn(y + 2)
-    s_y2 = [
-        cp.remote(sh.at[:, 0:2, lo, z], sh.at[:, 0:2, lo, z], at(0, 1)),
-        cp.remote(sh.at[:, 2:4, hi, z], sh.at[:, 2:4, hi, z], at(0, -1)),
-    ]
-    s_z += [cp.remote(sh.at[:, :, v, z], sh.at[:, :, v, z], at(0, 0, 1)) for v in (lo, hi)]
-    d_step(1)
-    home_in(1)
-    x_step(0, 0, 2)
-    y_step(0, 0)
-    home_in(2)
-    x_step(0, 1, 2)
-    y_step(0, 1)
-    home_in(3)
-    home_mid()
-    x_step(0, 2, 2)
-    y_step(0, 2)
-    home_out(0)
-    home_out(1)
-    x_step(0, 3, 2)
-    y_step(0, 3)
-    d_step(2)
-    dx_step(0)
-    home_out(2)
-    home_out(3)
-    own2 = exchange(pack2, got2, groups)
-    for c in s_y2:
-        c.wait_recv()
-    s_z.append(cp.remote(sh.at[:, :, opp, z], sh.at[:, :, opp, z], at(0, 0, 1)))
-    x_step(1, 0, 0)
-    x_step(1, 1, 0)
-    spread_y(0)
-    dx_step(1)
-    x_step(1, 2, 0)
-    x_step(1, 3, 0)
-    dx_step(2)
-    x_step(1, 0, 1)
-    x_step(1, 1, 1)
-    dx_step(3)
-    d_z = [cp.remote(xd.at[r, 2], hd.at[y, r], at(0, 0, 1)) for r in (0, 1)]
-    forward_y(0)
-    x_step(1, 2, 1)
-    x_step(1, 3, 1)
-    for c in t_t[:1] + [t_fwd2] + s_z:
-        c.wait_recv()
-    d_y = []
-    for r in (0, 1):
-        d_z[r].wait_recv()
-        choose(fz, xd.shape[2], 16, lambda i, r=r: xd[r, 2, i], hd.at[y, r])
-        d_y.append([cp.remote(hd.at[y, r], hd.at[y, r], at(0, d)) for d in (1, -1)])
-    shared_in(0)
-    shared_in(1)
-    x_step(1, 0, 2)
-    y_step(1, 0)
-    shared_in(2)
-    shared_in(3)
-    shared_mid()
-    x_step(1, 1, 2)
-    y_step(1, 1)
-    d_y[0][0].wait_recv()
-    d_y[1][1].wait_recv()
-    d_y2 = [
-        cp.remote(hd.at[lo, 0], hd.at[lo, 0], at(0, 1)),
-        cp.remote(hd.at[hi, 1], hd.at[hi, 1], at(0, -1)),
-    ]
-    shared_out(0)
-    shared_out(1)
-    x_step(1, 2, 2)
-    y_step(1, 2)
-    shared_out(2)
-    shared_out(3)
-    x_step(1, 3, 2)
-    y_step(1, 3)
-    home_back()
-    spread_y(1)
-    hot_arrived(0)
-    for k in range(4):
-        hot_in(0, k)
-    forward_y(1)
-    for c in c_x:
-        c.wait_recv()
-    hot_arrived(1)
-    for k in range(4):
-        hot_in(1, k)
-    d_y[0][1].wait_recv()
-    d_y[1][0].wait_recv()
-    for c in d_y2:
-        c.wait_recv()
-    for d in range(NX):
+    def send_back():
+        c_of["own2"] = exchange(pack2, got2, groups)
+
+    def shared_first():
+        cp.got(*c_of["sh_z"])
+        shared_in(0)
+
+    d_z, d_y, d_y2 = [], [], []
+
+    def d_z_send():
+        d_z.extend(cp.remote(xd.at[r, 2], hd.at[y, r], at(0, 0, 1)) for r in (0, 1))
+
+    def d_spread():
+        for r in (0, 1):
+            d_z[r].wait_recv()
+            choose(fz, xd.shape[2], 16, lambda i, r=r: xd[r, 2, i], hd.at[y, r])
+            d_y.append([cp.remote(hd.at[y, r], hd.at[y, r], at(0, d)) for d in (1, -1)])
+
+    def d_forward():
+        cp.got(d_y[0][0], d_y[1][1])
+        d_y2.append(cp.remote(hd.at[lo, 0], hd.at[lo, 0], at(0, 1)))
+        d_y2.append(cp.remote(hd.at[hi, 1], hd.at[hi, 1], at(0, -1)))
+
+    def hot_part(h):
+        hot_arrived(h)
+        for k in range(4):
+            hot_in(h, k)
+
+    def end():
+        cp.got(*c_of["coef"], d_y[0][1], d_y[1][0], *d_y2)
+
+    tasks = {
+        "tok0": own_tokens, "tokx": quad_tokens, "tt": quad_across, "tf": quad_relay,
+        "tq": quad_done, "own0": own_loads, "df": d_first, "dz0": d_z_send, "dy1": d_spread,
+        "dy2": d_forward, "sx": sh_x, "s1": sh_1, "s2": sh_2, "s3": sh_3, "route": route,
+        "pack": pack, "wts": weights, "unpack": unpack_rows, "hm": home_mid, "ex2": send_back,
+        "si0": shared_first, "sm": shared_mid, "hb": home_back, "end": end,
+    }
+    for name in ORDER:
+        if name in tasks:
+            tasks[name]()
+            continue
+        kind, at_ = name.rstrip("0123456789"), [int(c) for c in name.lstrip("abcdefghijklmnopqrstuvwxyz")]
+        if kind == "xf":
+            x_first(at_[0], at_[1:])
+        else:
+            {
+                "x": x_step, "y": y_step, "sy": spread_y, "fy": forward_y, "hot": hot_part,
+                "d": d_step, "dx": dx_step, "hi": home_in, "ho": home_out,
+                "si": shared_in, "so": shared_out,
+            }[kind](*at_)
+
+    first, rest = slice(0, SPLIT), slice(SPLIT, quarter)
+    to_c, by_x, by_z = {}, [], {}
+    order = (2, 1, 3, 0)
+    for d in order:
         a = slice(d * n, (d + 1) * n)
-        hot_hid[a] = (
-            silu(acc_g[a]) * acc_u[a] * as_col(coefs[d, 0:1])
-        ).astype(bf)
-
-    order = (2, 1, 3, 0)
-    to_c = {}
-    for d in order:
+        hot_hid[a] = (silu(acc_g[a]) * acc_u[a] * as_col(coefs[d, 0:1])).astype(bf)
         for q in range(4):
             lanes = slice(q * quarter, (q + 1) * quarter)
             wd = hd[:, :, :, lanes].reshape(cols, quarter)
-            psum[d, q] = psum[d, q] + dot(hot_hid[d * n : (d + 1) * n], wd)
-        to_core[d, :, 0:quarter] = psum[d, 1 - core].astype(bf)
-        to_core[d, :, quarter:] = psum[d, 3 - core].astype(bf)
+            psum[d, q] = psum[d, q] + dot(hot_hid[a], wd)
+        to_core[d, 0] = psum[d, 1 - core].astype(bf)
+        to_core[d, 1] = psum[d, 3 - core].astype(bf)
         to_c[d] = cp.remote(to_core.at[d], from_core.at[d], other)
-    to_x = []
+
+    def on_chip(d, side, lanes):
+        return psum[d, 2 * side + core, :, lanes] + from_core[d, side, :, lanes].astype(f32)
+
     for d in order:
         to_c[d].wait_recv()
         if d:
-            for i, q in enumerate((core, 2 + core)):
-                lanes = slice(i * quarter, (i + 1) * quarter)
-                mid[d - 1, :, lanes] = (psum[d, q] + from_core[d, :, lanes].astype(f32)).astype(bf)
-            to_x.append(cp.remote(mid.at[d - 1], from_x.at[d - 1], at(d)))
-    for c in to_x:
+            for side in (0, 1):
+                mid[d, side, :, first] = on_chip(d, side, first).astype(bf)
+            by_x.append(cp.remote(mid.at[d, :, :, first], from_x.at[d - 1], at(d)))
+        mid[d, 1 - z_hi, :, rest] = on_chip(d, 1 - z_hi, rest).astype(bf)
+        by_z[d] = cp.remote(mid.at[d, 1 - z_hi, :, rest], from_zb.at[d], across)
+    by_xb = []
+    for d in order[:3]:
+        by_z[d].wait_recv()
+        mid_b[d - 1] = (on_chip(d, z_hi, rest) + from_zb[d].astype(f32)).astype(bf)
+        by_xb.append(cp.remote(mid_b.at[d - 1], from_xb.at[d - 1], at(d)))
+    for c in by_x:
         c.wait_recv()
 
     def total(side):
-        lanes = of_quarter(side)
-        v = psum[0, 2 * side + core] + from_core[0, :, lanes].astype(f32)
+        v = on_chip(0, side, first)
         for i in range(3):
-            v += from_x[i, :, lanes].astype(f32)
+            v += from_x[i, side].astype(f32)
         return v
 
     half[...] = total(1 - z_hi).astype(bf)
     last = cp.remote(half, from_z, across)
     own_total = total(z_hi)
+    by_z[0].wait_recv()
+    v = on_chip(0, z_hi, rest) + from_zb[0].astype(f32)
+    for c in by_xb:
+        c.wait_recv()
+    for i in range(3):
+        v += from_xb[i].astype(f32)
+    out[:, rest] = v
     last.wait_recv()
-    out[...] = (mask[...].astype(f32) * (own_total + from_z[...].astype(f32))).astype(out.dtype)
+    out[:, first] = own_total + from_z[...].astype(f32)
     for c in cp.started:
         c.wait_send()
     exchanged(pack1, got1, 0, True)
@@ -557,15 +595,13 @@
     rows, cols = d // NY, h // NX
     part = cols // (2 * NY)
     groups = NX * NY * NZ
-    sh_own = jnp.stack([sh_gate, sh_up, sh_down.T])
     any_spec = pl.BlockSpec(memory_space=pl.ANY)
     vmem = pl.BlockSpec(memory_space=pltpu.VMEM)
     blocks = pltpu.VMEM((groups, 16, quarter), bf)
-    return pl.pallas_call(
+    summed = pl.pallas_call(
         layer_kernel,
-        out_shape=jax.ShapeDtypeStruct((n, quarter), bf),
-        in_specs=[pl.BlockSpec(memory_space=pltpu.SMEM), any_spec, vmem, vmem, vmem]
-        + [any_spec] * 4,
+        out_shape=jax.ShapeDtypeStruct((n, quarter), f32),
+        in_specs=[pl.BlockSpec(memory_space=pltpu.SMEM), any_spec, vmem, vmem] + [any_spec] * 6,
         out_specs=vmem,
         scratch_shapes=[
             pltpu.VMEM((NY, rows, h), bf),
@@ -580,7 +616,7 @@
             pltpu.VMEM((d, cols), bf),
             pltpu.VMEM((d, cols), bf),
             pltpu.VMEM((NY, 2, part, d), bf),
-            pltpu.VMEM((3, NX, NY, NZ, sh_own.shape[1], cols), bf),
+            pltpu.VMEM((3, NX, NY, NZ, sh_gate.shape[0], cols), bf),
             pltpu.VMEM((NX, n, d), bf),
             pltpu.VMEM((NX, 8, n), f32),
             blocks, blocks, blocks, blocks,
@@ -593,16 +629,20 @@
             pltpu.VMEM((NX * n, cols), bf),
             pltpu.VMEM((NX * n, cols), bf),
             pltpu.VMEM((NX, NT, n, quarter), f32),
-            pltpu.VMEM((NX, n, 2 * quarter), bf),
-            pltpu.VMEM((NX, n, 2 * quarter), bf),
-            pltpu.VMEM((3, n, 2 * quarter), bf),
-            pltpu.VMEM((3, n, 2 * quarter), bf),
-            pltpu.VMEM((n, quarter), bf),
-            pltpu.VMEM((n, quarter), bf),
+            pltpu.VMEM((NX, 2, n, quarter), bf),
+            pltpu.VMEM((NX, 2, n, quarter), bf),
+            pltpu.VMEM((NX, 2, n, quarter), bf),
+            pltpu.VMEM((3, 2, n, SPLIT), bf),
+            pltpu.VMEM((n, SPLIT), bf),
+            pltpu.VMEM((n, SPLIT), bf),
+            pltpu.VMEM((NX, n, quarter - SPLIT), bf),
+            pltpu.VMEM((3, n, quarter - SPLIT), bf),
+            pltpu.VMEM((3, n, quarter - SPLIT), bf),
             pltpu.VMEM((n, 128), f32),
             pltpu.VMEM((n, 128), f32),
-            pltpu.SemaphoreType.DMA((140,)),
-            pltpu.SemaphoreType.DMA((140,)),
+            pltpu.VMEM((n, 128), jnp.int32),
+            pltpu.SemaphoreType.DMA((SENDS,)),
+            pltpu.SemaphoreType.DMA((SENDS,)),
             pltpu.SemaphoreType.DMA((16,)),
             pltpu.SemaphoreType.DMA((2 * groups,)),
             pltpu.SemaphoreType.DMA((2 * groups,)),
@@ -611,9 +651,10 @@
             collective_id=0, has_side_effects=True, vmem_limit_bytes=62 * 2**20
         ),
     )(
-        scalars, tokens, slot, mask.reshape(n, 1), router_weight,
-        exp_gate[0], exp_up[0], exp_down[0].reshape(NX, NY, 2, part, d), sh_own,
+        scalars, tokens, slot.reshape(1, n), router_weight.T,
+        exp_gate[0], exp_up[0], exp_down[0].reshape(NX, NY, 2, part, d), sh_gate, sh_up, sh_down.T,
     )
+    return (mask.astype(f32)[:, None] * summed).astype(bf)
 
 
 def solution(mesh):

time: 216 us -> 185 us (0.86)
  Pallas kernels: 206 us -> 181 us
  local copies, waits for them, and re-layouts: 6.35 us -> 0 us
    pallas_call x1, Pallas kernels: 206 us -> 181 us  [local(): pl.pallas_call(layer_kernel, out_shape=jax.ShapeDtypeStruct((n, quarter),...]
    unnamed x3 -> x0, local copies, waits for them, and re-layouts: 4.98 us -> none
    convert_element_type x0 -> x2, other arithmetic: none -> 2.38 us  [local(): return (mask.astype(f32)[:, None] * summed).astype(bf)]
where the time goes in v3:
time: 185 us
  Pallas kernels  181 us (98%)
  other arithmetic  3.05 us (2%)
    pallas_call x1, Pallas kernels, local(): pl.pallas_call(layer_kernel, out_shape=jax.ShapeDtypeStruct((n, quarter),...  181 us

profile of v3, /device:TPU:1, one launch (start us, length us, event | category | flops | bytes accessed | tf_op | source)
XLA Modules:
  0.0 184.6 jit_solution(15197433716067504731)
XLA Ops:
  0.7 0.7 pad_add_fusion.scalars
  1.4 0.7 convert_element_type.4
  2.0 180.9 %shard_map.109 = f32[128,640]{1,0:T(8,128)} custom-call(s32[4]{0:T(128)} %pad_add_fusion.scalars, bf16[128,640]{1,0:T(8,128)(2,1)} %tok.1, s32[1,128]{1,0:T(1,128)} %bitcast.19, bf16[32,2560]{1,0:T(8,128)(2,1)} %bitcast.17, bf16[2560,1024]{1,0:T(8,128)(2,1)} %bitcast.14, bf16[2560,1024]{1,0:T(8,128)(2,1)} %bitcast.15, bf16[4,4,2,32,2560]{4,3,2,1,0:T(8,128)(2,1)} %bitcast.16, ...), custom_call_target="tpu_custom_call" | custom-call | tf_op jit(solution)/shard_map/pallas_call | solution.py:601
  182.9 1.7 multiply_convert_fusion

commit v4 on v3

--- a/solution.py
+++ b/solution.py
@@ -8,20 +8,20 @@
 MESH = pl.DeviceIdType.MESH
 NX, NY, NZ, NT, CAP = 4, 4, 2, 4, 4
 
-PARTS = ((0, 256), (256, 256), (512, 128))
+PARTS = ((0, 384), (384, 128), (512, 128))
 SPLIT = 384
 SENDS = 240
 ORDER = (
-    "tok0", "df", "own0", "tokx", "sx", "route", "pack", "wts", "tt", "s1", "d0", "xf00", "xf01",
-    "xf03", "unpack", "x000", "hi0", "hi1", "x010", "hi2", "hi3", "x030", "hm", "tf", "ho0", "x001",
-    "ho1", "ho2", "x011", "ho3", "s2", "ex2", "x031", "tq", "x002", "y00", "x012", "d1", "xf10",
-    "xf02", "s3", "x032", "xf11", "x100", "x020", "x110", "y01", "x101", "x021", "x111", "x102",
-    "y10", "xf12", "x022", "d2", "dx0", "x112", "y02", "si0", "x120", "si1", "y11", "si2", "dx1",
-    "y03", "si3", "xf20", "sm", "x121", "so0", "so1", "dx2", "so2", "so3", "hb", "x122", "y12",
-    "sy0", "xf13", "x200", "dx3", "dz0", "xf22", "xf21", "x130", "x201", "fy0", "x220", "x210",
-    "dy1", "x131", "hot0", "x202", "y20", "x221", "x211", "dy2", "xf23", "x132", "y13", "x222",
-    "x212", "y21", "x230", "y22", "x231", "sy1", "x232", "y23", "fy1", "sy2", "hot1", "fy2", "hot2",
-    "end",
+    "tok0", "df", "tokx", "own0", "own1t", "pack", "sx", "route", "wts", "tt", "xf00", "xf01", "s1",
+    "d0", "unpack", "x000", "tf", "xf02", "x010", "tq", "x001", "s2", "x020", "rf", "x011", "hi0",
+    "hi1", "hi2", "hi3", "d1", "x002", "y00", "x021", "hm", "ho0", "ho1", "s3", "xf03", "ho2",
+    "x012", "ho3", "hr1", "xf10", "x022", "xf20", "hr2", "xf11", "xf21", "x030", "x100", "x200",
+    "x110", "d2", "dx0", "x210", "y01", "si0", "x031", "x101", "si1", "si2", "si3", "y02", "x201",
+    "x111", "sm", "so0", "x211", "so1", "so2", "so3", "x032", "y03", "x102", "y10", "dx1", "ex2",
+    "x202", "y20", "x212", "x112", "y11", "xf12", "xf22", "dx2", "y21", "sy0", "x120", "x220", "hb",
+    "xf13", "xf23", "dx3", "dz0", "fy0", "x121", "x221", "x130", "x230", "x122", "y12", "x222",
+    "y22", "dy1", "x131", "hot0", "x231", "x132", "y13", "dy2", "x232", "y23", "sy1", "sy2", "fy1",
+    "fy2", "hot1", "hot2", "end",
 )
 
 
@@ -106,6 +106,7 @@
     pack1, got1, pack2, got2, rows_in, home_g, home_u, home_hid,
     acc_g, acc_u, sh_hid, hot_hid, psum, to_core, from_core, mid, from_x, half, from_z, from_zb, mid_b, from_xb,
     w_cols, target_cols, expert_cols,
+    tok_here, home_part, home_send, home_core, home_half, home_z, back,
     send, recv, local, a2a_send, a2a_recv,
 ):
     x, y, z = coords()
@@ -286,17 +287,30 @@
         eye = iota((n, n), 0) == iota((n, n), 1)
         return jnp.sum(jnp.where(eye, row, 0.0), axis=1, keepdims=True)
 
-    blocks_at_once = n // 16
-
-    def packed(c, q, key):
+    groups_here = NX * NY * NZ
+
+    depth = pack1.shape[1]
+    tiles = quarter // 128
+
+    def packed(c, i, key):
         r = iota((n, n), 0) + c * n
-        of = (r // 16) * 4 + r % 4
-        return ((of.astype(f32) == key) & ((r // 4) % 4 == q)).astype(bf)
-
-    def unpacked(q, key):
-        r = iota((n, 4 * n), 1)
-        of = (r // 16) * 4 + r % 4
-        return ((of.astype(f32) == key) & ((r // 4) % 4 == q)).astype(bf)
+        of = (r // depth) * CAP + r % CAP
+        return ((of.astype(f32) == key) & ((r % depth) // CAP == i)).astype(bf)
+
+    def pack_into(into, v, key):
+        for c in range(groups_here * depth // n):
+            acc = jnp.zeros((n, 128), f32)
+            for i in range(tiles):
+                acc += dot(packed(c, i, key), v[:, i * 128 : (i + 1) * 128])
+            into[c * n // depth : (c + 1) * n // depth] = acc.astype(bf).reshape(
+                n // depth, depth, 128
+            )
+
+    def unpacked(flat, i, key):
+        r = iota((n, groups_here * depth), 1)
+        of = (r // depth) * CAP + r % CAP
+        pick = ((of.astype(f32) == key) & ((r % depth) // CAP == i)).astype(bf)
+        return dot(pick, flat)
 
     mine = of_quarter(t)
     theirs = of_quarter(across_t)
@@ -305,6 +319,7 @@
     def own_tokens():
         c_of["peer"] = [cp.remote(tok, tk.at[0, :, mine], d) for d in (other, across)]
         c_of["own"] = cp.here(tok, tk.at[0, :, mine])
+        c_of["here"] = cp.here(tok, tok_here)
 
     def quad_tokens():
         c_of["quad"] = [cp.remote(tok, tk.at[(4 - d) % 4, :, mine], at(d)) for d in (2, 1, -1)]
@@ -363,7 +378,8 @@
         cp.got(*c_of["sh_y2"])
         c_of["sh_z"].append(sh_to(sh.at[:, :, opp, z], at(0, 0, 1)))
 
-    def route():
+    def positions():
+        cp.placed(c_of["here"])
         ids_row = slot[...].astype(f32)
         ids_f = as_col(ids_row)
         ids = ids_f.astype(jnp.int32)
@@ -374,24 +390,19 @@
         target_cols[...] = jnp.broadcast_to(target, target_cols.shape)
         expert = jnp.where(spare, hot, ids >> 1)
         expert_cols[...] = jnp.broadcast_to(expert, expert_cols.shape)
+
+    def relay():
         cp.placed(c_of["own"])
         cp.got(c_of["peer"][1])
         a = tk.at[0, :, theirs]
         c_of["relay"] = cp.remote(a, a, other)
 
     def pack():
+        pack_into(pack1, tok_here, as_row(target_cols[:, 0:1]))
+        c_of["own1"] = exchange(pack1, got1, 0)
+
+    def weights():
         cp.got(c_of["peer"][0], c_of["relay"])
-        target_row = as_row(target_cols[:, 0:1])
-        for c in range(4):
-            acc = jnp.zeros((n, quarter), f32)
-            for q in range(4):
-                acc += dot(packed(c, q, target_row), tk[0, :, q * quarter : (q + 1) * quarter])
-            pack1[c * blocks_at_once : (c + 1) * blocks_at_once] = acc.astype(bf).reshape(
-                blocks_at_once, 16, quarter
-            )
-        c_of["own1"] = exchange(pack1, got1, 0)
-
-    def weights():
         logits = lax.dot_general(
             tk[0], router[...], (((1,), (1,)), ((), ())), preferred_element_type=f32
         )
@@ -405,12 +416,22 @@
     def unpack_rows():
         exchanged(pack1, got1, 0, False)
         cp.placed(c_of["own1"])
-        flat = got1[...].reshape(4 * n, quarter)
+        flat = got1[...].reshape(groups_here * depth, 128)
         key = iota((n, 1), 0).astype(f32)
-        for q in range(4):
-            rows_in[:, q * quarter : (q + 1) * quarter] = dot(unpacked(q, key), flat).astype(bf)
+        for i in range(tiles):
+            lanes = pl.ds(pl.multiple_of(t * quarter + i * 128, 128), 128)
+            rows_in[:, lanes] = unpacked(flat, i, key).astype(bf)
+        a = rows_in.at[:, mine]
+        c_of["rows"] = [cp.remote(a, a, d) for d in (other, across)]
+
+    def rows_relay():
+        cp.got(c_of["rows"][1])
+        a = rows_in.at[:, theirs]
+        c_of["rows_relay"] = cp.remote(a, a, other)
 
     def home_in(j):
+        if j == 0:
+            cp.got(c_of["rows"][0], c_of["rows_relay"])
         for acc, own, sign in ((home_g, own_g, 1), (home_u, own_u, -1)):
             cp.placed(own_copy[0 if sign == 1 else 1, j])
             a = rows_in[:, pl.ds(pl.multiple_of(block(sign, j) * rows, rows), rows)]
@@ -427,21 +448,34 @@
         for i in range(NX):
             wd = own_d[i, :, :, :, lanes].reshape(cols, quarter)
             v += dot(home_hid[:, i * cols : (i + 1) * cols], wd)
-        acc_rows = v.astype(bf)
+        home_part[q] = v
+
+    def home_sum_core():
+        for side in (0, 1):
+            home_send[side] = home_part[2 * side + 1 - core].astype(bf)
+        c_of["home_core"] = cp.remote(home_send, home_core, other)
+
+    def home_sum_across():
+        cp.got(c_of["home_core"])
+        v = home_part[2 * (1 - z_hi) + core] + home_core[1 - z_hi].astype(f32)
+        home_half[...] = v.astype(bf)
+        c_of["home_z"] = cp.remote(home_half, home_z, across)
+
+    def send_back():
+        cp.got(c_of["home_z"])
+        v = home_part[2 * z_hi + core] + home_core[z_hi].astype(f32) + home_z[...].astype(f32)
         row = iota((1, n), 1).astype(f32)
-        for c in range(4):
-            a = slice(c * blocks_at_once, (c + 1) * blocks_at_once)
-            p = dot(packed(c, q, row), acc_rows).astype(bf).reshape(blocks_at_once, 16, quarter)
-            pack2[a] = p if q == 0 else pack2[a] + p
+        pack_into(pack2, v.astype(bf), row)
+        c_of["own2"] = exchange(pack2, got2, groups)
 
     def home_back():
         exchanged(pack2, got2, groups, False)
         cp.placed(c_of["own2"])
-        flat = got2[...].reshape(4 * n, quarter)
+        flat = got2[...].reshape(groups_here * depth, 128)
         key = target_cols[:, 0:1]
-        for q in range(4):
-            back = dot(unpacked(q, key), flat)
-            psum[0, q] = psum[0, q] + w_cols[:, 0:1] * back
+        for i in range(tiles):
+            lanes = slice(i * 128, (i + 1) * 128)
+            back[:, lanes] = w_cols[:, 0:1] * unpacked(flat, i, key)
 
     def quad_in(lanes, w_gate, w_up, first):
         a = tk[:, :, lanes].reshape(NX * n, -1)
@@ -470,9 +504,6 @@
         lanes = slice(k * rows + off, k * rows + off + r)
         quad_in(lanes, hg[lanes], hu[lanes], h == 0 and k == 0)
 
-    def send_back():
-        c_of["own2"] = exchange(pack2, got2, groups)
-
     def shared_first():
         cp.got(*c_of["sh_z"])
         shared_in(0)
@@ -504,7 +535,8 @@
     tasks = {
         "tok0": own_tokens, "tokx": quad_tokens, "tt": quad_across, "tf": quad_relay,
         "tq": quad_done, "own0": own_loads, "df": d_first, "dz0": d_z_send, "dy1": d_spread,
-        "dy2": d_forward, "sx": sh_x, "s1": sh_1, "s2": sh_2, "s3": sh_3, "route": route,
+        "dy2": d_forward, "sx": sh_x, "s1": sh_1, "s2": sh_2, "s3": sh_3, "own1t": positions, "route": relay, "rf": rows_relay, "hr1": home_sum_core,
+        "hr2": home_sum_across,
         "pack": pack, "wts": weights, "unpack": unpack_rows, "hm": home_mid, "ex2": send_back,
         "si0": shared_first, "sm": shared_mid, "hb": home_back, "end": end,
     }
@@ -563,9 +595,9 @@
 
     half[...] = total(1 - z_hi).astype(bf)
     last = cp.remote(half, from_z, across)
-    own_total = total(z_hi)
+    own_total = total(z_hi) + back[:, first]
     by_z[0].wait_recv()
-    v = on_chip(0, z_hi, rest) + from_zb[0].astype(f32)
+    v = on_chip(0, z_hi, rest) + from_zb[0].astype(f32) + back[:, rest]
     for c in by_xb:
         c.wait_recv()
     for i in range(3):
@@ -597,7 +629,8 @@
     groups = NX * NY * NZ
     any_spec = pl.BlockSpec(memory_space=pl.ANY)
     vmem = pl.BlockSpec(memory_space=pltpu.VMEM)
-    blocks = pltpu.VMEM((groups, 16, quarter), bf)
+    depth = -(-CAP * quarter // 128 // 16) * 16
+    blocks = pltpu.VMEM((groups, depth, 128), bf)
     summed = pl.pallas_call(
         layer_kernel,
         out_shape=jax.ShapeDtypeStruct((n, quarter), f32),
@@ -641,6 +674,13 @@
             pltpu.VMEM((n, 128), f32),
             pltpu.VMEM((n, 128), f32),
             pltpu.VMEM((n, 128), jnp.int32),
+            pltpu.VMEM((n, quarter), bf),
+            pltpu.VMEM((NT, n, quarter), f32),
+            pltpu.VMEM((2, n, quarter), bf),
+            pltpu.VMEM((2, n, quarter), bf),
+            pltpu.VMEM((n, quarter), bf),
+            pltpu.VMEM((n, quarter), bf),
+            pltpu.VMEM((n, quarter), f32),
             pltpu.SemaphoreType.DMA((SENDS,)),
             pltpu.SemaphoreType.DMA((SENDS,)),
             pltpu.SemaphoreType.DMA((16,)),

time: 185 us -> 177 us (0.957)
  Pallas kernels: 181 us -> 173 us
    pallas_call x1, Pallas kernels: 181 us -> 173 us  [local(): pl.pallas_call(layer_kernel, out_shape=jax.ShapeDtypeStruct((n, quarter),...]
where the time goes in v4:
time: 177 us
  Pallas kernels  173 us (98%)
  other arithmetic  3.05 us (2%)
    pallas_call x1, Pallas kernels, local(): pl.pallas_call(layer_kernel, out_shape=jax.ShapeDtypeStruct((n, quarter),...  173 us

profile of v4, /device:TPU:1, one launch (start us, length us, event | category | flops | bytes accessed | tf_op | source)
XLA Modules:
  0.0 177.1 jit_solution(15449546435043157673)
XLA Ops:
  0.7 0.7 pad_add_fusion.scalars
  1.4 0.7 convert_element_type.4
  2.0 173.4 %shard_map.109 = f32[128,640]{1,0:T(8,128)} custom-call(s32[4]{0:T(128)} %pad_add_fusion.scalars, bf16[128,640]{1,0:T(8,128)(2,1)} %tok.1, s32[1,128]{1,0:T(1,128)} %bitcast.19, bf16[32,2560]{1,0:T(8,128)(2,1)} %bitcast.17, bf16[2560,1024]{1,0:T(8,128)(2,1)} %bitcast.14, bf16[2560,1024]{1,0:T(8,128)(2,1)} %bitcast.15, bf16[4,4,2,32,2560]{4,3,2,1,0:T(8,128)(2,1)} %bitcast.16, ...), custom_call_target="tpu_custom_call" | custom-call | tf_op jit(solution)/shard_map/pallas_call | solution.py:634
  175.4 1.7 multiply_convert_fusion

commit v5 on v4

--- a/solution.py
+++ b/solution.py
@@ -12,16 +12,16 @@
 SPLIT = 384
 SENDS = 240
 ORDER = (
-    "tok0", "df", "tokx", "own0", "own1t", "pack", "sx", "route", "wts", "tt", "xf00", "xf01", "s1",
-    "d0", "unpack", "x000", "tf", "xf02", "x010", "tq", "x001", "s2", "x020", "rf", "x011", "hi0",
-    "hi1", "hi2", "hi3", "d1", "x002", "y00", "x021", "hm", "ho0", "ho1", "s3", "xf03", "ho2",
-    "x012", "ho3", "hr1", "xf10", "x022", "xf20", "hr2", "xf11", "xf21", "x030", "x100", "x200",
-    "x110", "d2", "dx0", "x210", "y01", "si0", "x031", "x101", "si1", "si2", "si3", "y02", "x201",
-    "x111", "sm", "so0", "x211", "so1", "so2", "so3", "x032", "y03", "x102", "y10", "dx1", "ex2",
-    "x202", "y20", "x212", "x112", "y11", "xf12", "xf22", "dx2", "y21", "sy0", "x120", "x220", "hb",
-    "xf13", "xf23", "dx3", "dz0", "fy0", "x121", "x221", "x130", "x230", "x122", "y12", "x222",
-    "y22", "dy1", "x131", "hot0", "x231", "x132", "y13", "dy2", "x232", "y23", "sy1", "sy2", "fy1",
-    "fy2", "hot1", "hot2", "end",
+    "df", "tok0", "tokx", "sx", "xf00", "own0", "own1t", "pack", "xf01", "route", "wts", "tt",
+    "xf02", "s1", "xf03", "d0", "x000", "unpack", "xf12", "xf10", "tf", "x010", "tq", "xf11",
+    "x020", "s2", "x030", "x001", "rf", "x120", "x100", "hi0", "hi1", "d1", "x011", "hi2", "x110",
+    "hi3", "s3", "hm", "ho0", "ho1", "ho2", "ho3", "hr1", "x021", "x031", "x002", "y00", "hr2",
+    "x121", "xf20", "x101", "d2", "dx0", "x012", "y01", "x111", "xf21", "si0", "si1", "x022", "si2",
+    "y02", "si3", "x032", "x122", "sm", "so0", "so1", "x102", "y03", "y10", "so2", "dx1", "x112",
+    "so3", "y11", "x200", "x210", "ex2", "dx2", "y12", "x201", "xf13", "xf22", "xf23", "sy0",
+    "x211", "hb", "dx3", "dz0", "x202", "y20", "fy0", "x130", "x220", "x230", "x212", "y21", "x131",
+    "x221", "dy1", "x231", "hot0", "x132", "y13", "x222", "y22", "x232", "dy2", "sy1", "y23", "fy1",
+    "sy2", "hot1", "fy2", "hot2", "end",
 )
 
 
@@ -557,7 +557,8 @@
     first, rest = slice(0, SPLIT), slice(SPLIT, quarter)
     to_c, by_x, by_z = {}, [], {}
     order = (2, 1, 3, 0)
-    for d in order:
+
+    def product(d):
         a = slice(d * n, (d + 1) * n)
         hot_hid[a] = (silu(acc_g[a]) * acc_u[a] * as_col(coefs[d, 0:1])).astype(bf)
         for q in range(4):
@@ -571,7 +572,7 @@
     def on_chip(d, side, lanes):
         return psum[d, 2 * side + core, :, lanes] + from_core[d, side, :, lanes].astype(f32)
 
-    for d in order:
+    def onward(d):
         to_c[d].wait_recv()
         if d:
             for side in (0, 1):
@@ -579,6 +580,12 @@
             by_x.append(cp.remote(mid.at[d, :, :, first], from_x.at[d - 1], at(d)))
         mid[d, 1 - z_hi, :, rest] = on_chip(d, 1 - z_hi, rest).astype(bf)
         by_z[d] = cp.remote(mid.at[d, 1 - z_hi, :, rest], from_zb.at[d], across)
+
+    product(order[0])
+    for i in (1, 2, 3):
+        product(order[i])
+        onward(order[i - 1])
+    onward(order[3])
     by_xb = []
     for d in order[:3]:
         by_z[d].wait_recv()

time: 177 us -> 176 us (level)
  no operation moved by 1% of the time
where the time goes in v5:
time: 176 us; the launch traced here: 175 us
  Pallas kernels  172 us (98%)
  other arithmetic  3.05 us (2%)
    pallas_call x1, Pallas kernels, local(): pl.pallas_call(layer_kernel, out_shape=jax.ShapeDtypeStruct((n, quarter),...  172 us

profile of v5, /device:TPU:1, one launch (start us, length us, event | category | flops | bytes accessed | tf_op | source)
XLA Modules:
  0.0 175.4 jit_solution(1701257833632177952)
XLA Ops:
  0.7 0.7 pad_add_fusion.scalars
  1.4 0.7 convert_element_type.4
  2.0 171.6 %shard_map.109 = f32[128,640]{1,0:T(8,128)} custom-call(s32[4]{0:T(128)} %pad_add_fusion.scalars, bf16[128,640]{1,0:T(8,128)(2,1)} %tok.1, s32[1,128]{1,0:T(1,128)} %bitcast.19, bf16[32,2560]{1,0:T(8,128)(2,1)} %bitcast.17, bf16[2560,1024]{1,0:T(8,128)(2,1)} %bitcast.14, bf16[2560,1024]{1,0:T(8,128)(2,1)} %bitcast.15, bf16[4,4,2,32,2560]{4,3,2,1,0:T(8,128)(2,1)} %bitcast.16, ...), custom_call_target="tpu_custom_call" | custom-call | tf_op jit(solution)/shard_map/pallas_call | solution.py:641
  173.7 1.7 multiply_convert_fusion

commit v6 on v5

--- a/solution.py
+++ b/solution.py
@@ -213,11 +213,6 @@
             a = hot_rows(hb, h, turn(y - sign))
             far2[h, s] = cp.remote(a, a, at(0, sign))
 
-    def hot_arrived(h):
-        for s in (0, 1):
-            near[h, s][1].wait_recv()
-            far2[h, s].wait_recv()
-
     d_copy, dx_copy = {}, {}
 
     def d_first():
@@ -499,10 +494,10 @@
         )
         psum[:, q] = v.reshape(NX, n, quarter)
 
-    def hot_in(h, k):
+    def hot_in(h, v, is_first):
         off, r = parts[h]
-        lanes = slice(k * rows + off, k * rows + off + r)
-        quad_in(lanes, hg[lanes], hu[lanes], h == 0 and k == 0)
+        lanes = pl.ds(pl.multiple_of(v * rows + off, 128), r)
+        quad_in(lanes, hg[lanes], hu[lanes], is_first)
 
     def shared_first():
         cp.got(*c_of["sh_z"])
@@ -525,9 +520,14 @@
         d_y2.append(cp.remote(hd.at[hi, 1], hd.at[hi, 1], at(0, -1)))
 
     def hot_part(h):
-        hot_arrived(h)
-        for k in range(4):
-            hot_in(h, k)
+        hot_in(h, y, h == 0)
+        for c in (near[h, 0][1], near[h, 1][1]):
+            c.wait_recv()
+        hot_in(h, lo, False)
+        hot_in(h, hi, False)
+        for c in (far2[h, 0], far2[h, 1]):
+            c.wait_recv()
+        hot_in(h, opp, False)
 
     def end():
         cp.got(*c_of["coef"], d_y[0][1], d_y[1][0], *d_y2)
@@ -558,16 +558,19 @@
     to_c, by_x, by_z = {}, [], {}
     order = (2, 1, 3, 0)
 
+    def grown(d, a, q):
+        wd = hd[:, :, :, of_quarter(q)].reshape(cols, quarter)
+        return psum[d, q] + dot(hot_hid[a], wd)
+
     def product(d):
         a = slice(d * n, (d + 1) * n)
         hot_hid[a] = (silu(acc_g[a]) * acc_u[a] * as_col(coefs[d, 0:1])).astype(bf)
-        for q in range(4):
-            lanes = slice(q * quarter, (q + 1) * quarter)
-            wd = hd[:, :, :, lanes].reshape(cols, quarter)
-            psum[d, q] = psum[d, q] + dot(hot_hid[a], wd)
-        to_core[d, 0] = psum[d, 1 - core].astype(bf)
-        to_core[d, 1] = psum[d, 3 - core].astype(bf)
+        for side in (0, 1):
+            to_core[d, side] = grown(d, a, 2 * side + 1 - core).astype(bf)
         to_c[d] = cp.remote(to_core.at[d], from_core.at[d], other)
+        for side in (0, 1):
+            q = 2 * side + core
+            psum[d, q] = grown(d, a, q)
 
     def on_chip(d, side, lanes):
         return psum[d, 2 * side + core, :, lanes] + from_core[d, side, :, lanes].astype(f32)

time: 176 us -> 175 us (level)
  no operation moved by 1% of the time
where the time goes in v6:
time: 175 us; the launch traced here: 174 us
  Pallas kernels  171 us (98%)
  other arithmetic  3.05 us (2%)
    pallas_call x1, Pallas kernels, local(): pl.pallas_call(layer_kernel, out_shape=jax.ShapeDtypeStruct((n, quarter),...  171 us

profile of v6, /device:TPU:1, one launch (start us, length us, event | category | flops | bytes accessed | tf_op | source)
XLA Modules:
  0.0 174.4 jit_solution(12575852590751985092)
XLA Ops:
  0.7 0.7 pad_add_fusion.scalars
  1.4 0.7 convert_element_type.4
  2.0 170.6 %shard_map.109 = f32[128,640]{1,0:T(8,128)} custom-call(s32[4]{0:T(128)} %pad_add_fusion.scalars, bf16[128,640]{1,0:T(8,128)(2,1)} %tok.1, s32[1,128]{1,0:T(1,128)} %bitcast.19, bf16[32,2560]{1,0:T(8,128)(2,1)} %bitcast.17, bf16[2560,1024]{1,0:T(8,128)(2,1)} %bitcast.14, bf16[2560,1024]{1,0:T(8,128)(2,1)} %bitcast.15, bf16[4,4,2,32,2560]{4,3,2,1,0:T(8,128)(2,1)} %bitcast.16, ...), custom_call_target="tpu_custom_call" | custom-call | tf_op jit(solution)/shard_map/pallas_call | solution.py:644
  172.6 1.7 multiply_convert_fusion

commit v7 on v6

--- a/solution.py
+++ b/solution.py
@@ -141,7 +141,6 @@
     lax.fori_loop(1, groups, greet, 0)
     for d in (other, across):
         pl.semaphore_signal(barrier, inc=1, device_id=d, device_id_type=MESH)
-    pl.semaphore_wait(barrier, groups + 1)
     fx, fy, fz, hot = scalars[0], scalars[1], scalars[2], scalars[3]
 
     streams = ((gate, own_g, xg, yg, hg, 1), (up, own_u, xu, yu, hu, -1))
@@ -313,8 +312,6 @@
 
     def own_tokens():
         c_of["peer"] = [cp.remote(tok, tk.at[0, :, mine], d) for d in (other, across)]
-        c_of["own"] = cp.here(tok, tk.at[0, :, mine])
-        c_of["here"] = cp.here(tok, tok_here)
 
     def quad_tokens():
         c_of["quad"] = [cp.remote(tok, tk.at[(4 - d) % 4, :, mine], at(d)) for d in (2, 1, -1)]
@@ -540,7 +537,14 @@
         "pack": pack, "wts": weights, "unpack": unpack_rows, "hm": home_mid, "ex2": send_back,
         "si0": shared_first, "sm": shared_mid, "hb": home_back, "end": end,
     }
+    c_of["here"] = cp.here(tok, tok_here)
+    c_of["own"] = cp.here(tok, tk.at[0, :, mine])
+    own_loads()
+    positions()
+    pl.semaphore_wait(barrier, groups + 1)
     for name in ORDER:
+        if name in ("own0", "own1t"):
+            continue
         if name in tasks:
             tasks[name]()
             continue

time: 175 us -> 174 us (level)
  no operation moved by 1% of the time
where the time goes in v7:
time: 174 us
  Pallas kernels  170 us (98%)
  other arithmetic  3.05 us (2%)
    pallas_call x1, Pallas kernels, local(): pl.pallas_call(layer_kernel, out_shape=jax.ShapeDtypeStruct((n, quarter),...  170 us

profile of v7, /device:TPU:1, one launch (start us, length us, event | category | flops | bytes accessed | tf_op | source)
XLA Modules:
  0.0 174.3 jit_solution(14696304813419493484)
XLA Ops:
  0.7 0.7 pad_add_fusion.scalars
  1.4 0.7 convert_element_type.4
  2.0 170.5 %shard_map.109 = f32[128,640]{1,0:T(8,128)} custom-call(s32[4]{0:T(128)} %pad_add_fusion.scalars, bf16[128,640]{1,0:T(8,128)(2,1)} %tok.1, s32[1,128]{1,0:T(1,128)} %bitcast.19, bf16[32,2560]{1,0:T(8,128)(2,1)} %bitcast.17, bf16[2560,1024]{1,0:T(8,128)(2,1)} %bitcast.14, bf16[2560,1024]{1,0:T(8,128)(2,1)} %bitcast.15, bf16[4,4,2,32,2560]{4,3,2,1,0:T(8,128)(2,1)} %bitcast.16, ...), custom_call_target="tpu_custom_call" | custom-call | tf_op jit(solution)/shard_map/pallas_call | solution.py:648
  172.5 1.7 multiply_convert_fusion
